TPU v7x, 512 devices: a whole 4x4x16 slice. The times are simulated.
512 devices in a mesh: cells: 128 (over y, z, core), rep: 4 (over x).
Axes of the slice: x: 4, y: 4, z: 16, core: 2. Of those that a mesh axis runs over, the one named last changes fastest.
Arguments:
- particle_speeds: float32 [65536, 3, 128], P(('cells', 'rep')), may hold values from -6 to 6
- particle_diameters: float32 [65536, 128], P(('cells', 'rep')), may hold values from 0.5 to 2
- particle_kelvins: float32 [65536, 128], P(('cells', 'rep')), may hold values from -6 to 6
- unscaled_kernel_coefficients: bfloat16 [65536, 64, 128], P(('cells', 'rep')), may hold values from 0 to 1
- bundle_patch_ordinal: int32 [65536], P(('cells', 'rep')), may hold values from 0 to 255
- bundle_patch_custodian: int32 [65536], P(('cells', 'rep')), may hold values from 0 to 127, as said below
- busy_bundles_per_accelerator: int32 [512], P(('cells', 'rep')), may hold values from 64 to 128, as said below
- ambient_flow_quantities: bfloat16 [32768, 256], P('cells'), may hold values from -24 to 24
Outputs:
- advanced_motion_vector: float32 [65536, 3, 128], P(('cells', 'rep'))
- advanced_thermal_level: float32 [65536, 128], P(('cells', 'rep'))
- forcing_mesh_values: float32 [32768, 256], P(('cells', 'rep'))
Inputs may be any that keep to these rules, and one draw needn't show every extreme that they name: `bundle_patch_custodian`: counting all 128 blocks of one device, live or not, no owner is named more than 2 times; one owner, the same on every device, is named exactly 2 times by the live blocks of every device. `busy_bundles_per_accelerator`: some device has all 128 blocks live.
All inputs are finite; a program needn't handle non-finite values.
Results may differ from a plain program's by a relative error of at most 0.00061.
Values may be sent and summed in bfloat16 or wider, within the bound.
A program may use at most 64 MiB of HBM per device.

v0:
```python
import jax
import jax.numpy as jnp
from jax import lax
from jax.sharding import PartitionSpec as P

REYNOLDS_SCALE = 20.0
DRAG_SCALE = 1.0
HEAT_SCALE = 0.5
PRANDTL_ROOT = 0.9
LOADING = 0.2


def integrate_timestep(looked_up, tiles_here, parcel_velocity, parcel_diameter, parcel_heat):
    blocks_here = looked_up.shape[0]
    cells_block = tiles_here.shape[1]
    scale = 2.0 / cells_block
    cell_values = looked_up.reshape(blocks_here, 4, cells_block)
    sampled = (
        jnp.einsum("nck,nkp->ncp", cell_values, tiles_here, preferred_element_type=jnp.float32)
        * scale
    )
    gas_velocity = sampled[:, :3]
    warmth = sampled[:, 3]
    slip_velocity = gas_velocity - parcel_velocity
    slip_speed = jnp.sqrt(1.0 + jnp.sum(slip_velocity * slip_velocity, axis=1))
    reynolds = REYNOLDS_SCALE * parcel_diameter * slip_speed
    squared = parcel_diameter * parcel_diameter
    drag_rate = DRAG_SCALE * (1.0 + 0.15 * reynolds**0.687) / squared
    heat_rate = HEAT_SCALE * (2.0 + 0.6 * PRANDTL_ROOT * jnp.sqrt(reynolds)) / squared
    relocated_bundles = (parcel_velocity + drag_rate[:, None] * gas_velocity) / (
        1.0 + drag_rate[:, None]
    )
    particles_after_heating = (parcel_heat + heat_rate * warmth) / (1.0 + heat_rate)
    parcel_mass = LOADING * parcel_diameter * squared
    momentum_heat = jnp.concatenate(
        [
            -parcel_mass[:, None] * (relocated_bundles - parcel_velocity),
            (-parcel_mass * (particles_after_heating - parcel_heat))[:, None],
        ],
        axis=1,
    )
    rounded = momentum_heat.astype(jnp.bfloat16)
    coupling_terms = (
        jnp.einsum("ncp,nkp->nck", rounded, tiles_here, preferred_element_type=jnp.float32) * scale
    )
    return (
        relocated_bundles,
        particles_after_heating,
        coupling_terms.reshape(blocks_here, 4 * cells_block),
    )


def assign_slots(bundle_patch_custodian, busy_bundles_per_accelerator, owners_count, capacity):
    blocks_here = bundle_patch_custodian.shape[0]
    positions = jnp.arange(blocks_here, dtype=jnp.int32)
    active_groups = positions < busy_bundles_per_accelerator[0]
    earlier_same = (
        (bundle_patch_custodian[:, None] == bundle_patch_custodian[None, :])
        & (positions[None, :] < positions[:, None])
        & active_groups[None, :]
    )
    rank_in = jnp.sum(earlier_same.astype(jnp.int32), axis=1)
    slot_count = owners_count * capacity
    slot_of = jnp.where(active_groups, bundle_patch_custodian * capacity + rank_in, slot_count)
    holder = jnp.full((slot_count,), -1, jnp.int32).at[slot_of].set(positions, mode="drop")
    return (active_groups, jnp.minimum(slot_of, slot_count - 1), holder)


def deposit(coupling_terms, destination_patch, usable, custodian_patches):
    onehot = (
        (destination_patch[None, :] == jnp.arange(custodian_patches, dtype=jnp.int32)[:, None])
        & usable[None, :]
    ).astype(jnp.float32)
    return jnp.dot(
        onehot, coupling_terms, precision=lax.Precision.HIGHEST, preferred_element_type=jnp.float32
    )


def per_device(
    particle_speeds,
    particle_diameters,
    particle_kelvins,
    unscaled_kernel_coefficients,
    bundle_patch_ordinal,
    bundle_patch_custodian,
    busy_bundles_per_accelerator,
    ambient_flow_quantities,
):
    blocks_here = bundle_patch_custodian.shape[0]
    custodian_patches = ambient_flow_quantities.shape[0]
    owners_count = lax.axis_size("cells")
    capacity = max(2, (blocks_here + owners_count - 1) // owners_count)
    active_groups, slot_of, holder = assign_slots(
        bundle_patch_custodian, busy_bundles_per_accelerator, owners_count, capacity
    )
    filled = holder >= 0
    picked = jnp.maximum(holder, 0)
    sent_tiles = unscaled_kernel_coefficients[picked]
    spray_condition = jnp.concatenate(
        [particle_speeds, particle_diameters[:, None], particle_kelvins[:, None]], axis=1
    )[picked]
    labels = jnp.stack(
        [bundle_patch_ordinal[picked].astype(jnp.float32), filled.astype(jnp.float32)], axis=1
    )
    received_bundle_arrays = lax.all_to_all(
        sent_tiles, "cells", split_axis=0, concat_axis=0, tiled=True
    )
    received_particle_data, got_labels = (
        lax.all_to_all(spray_condition, "cells", split_axis=0, concat_axis=0, tiled=True),
        lax.all_to_all(labels, "cells", split_axis=0, concat_axis=0, tiled=True),
    )
    destination_patch = got_labels[:, 0].astype(jnp.int32)
    usable = got_labels[:, 1] > 0.5
    relocated_bundles, particles_after_heating, coupling_terms = integrate_timestep(
        ambient_flow_quantities[destination_patch],
        received_bundle_arrays,
        received_particle_data[:, :3],
        received_particle_data[:, 3],
        received_particle_data[:, 4],
    )
    partial_field = deposit(coupling_terms, destination_patch, usable, custodian_patches)
    returned = lax.all_to_all(
        jnp.concatenate([relocated_bundles, particles_after_heating[:, None]], axis=1),
        "cells",
        split_axis=0,
        concat_axis=0,
        tiled=True,
    )
    mine = returned[slot_of]
    moved_home = mine[:, :3]
    warmed_local_share = mine[:, 3]
    advanced_motion_vector = jnp.where(active_groups[:, None, None], moved_home, particle_speeds)
    advanced_thermal_level = jnp.where(active_groups[:, None], warmed_local_share, particle_kelvins)
    forcing_mesh_values = lax.psum_scatter(partial_field, "rep", scatter_dimension=0, tiled=True)
    return (advanced_motion_vector, advanced_thermal_level, forcing_mesh_values)


def solution(mesh):
    in_specs = (
        P(("cells", "rep"), None, None),
        P(("cells", "rep"), None),
        P(("cells", "rep"), None),
        P(("cells", "rep"), None, None),
        P(("cells", "rep")),
        P(("cells", "rep")),
        P(("cells", "rep")),
        P("cells", None),
    )
    out_specs = (
        P(("cells", "rep"), None, None),
        P(("cells", "rep"), None),
        P(("cells", "rep"), None),
    )
    return jax.shard_map(
        per_device, mesh=mesh, in_specs=in_specs, out_specs=out_specs, check_vma=False
    )
```

profile of v0, /device:TPU:1, one launch (start us, length us, event | category | flops | bytes accessed | tf_op | source)
XLA Modules:
  0.0 368.8 jit_solution(6535950039462396365)
XLA Ops:
  8.0 0.9 convert_reduce_fusion
  9.6 1.0 scatter_custom_fusion
  10.6 1.9 gather_fusion.1
  13.6 20.6 %all-to-all-start.1 = ((f32[128,2,2]{1,2,0:T(2,128)}), f32[128,2,2]{1,2,0:T(2,128)S(1)}, u32[]{:S(2)}, u32[]{:S(2)}) async-start(f32[128,2,2]{1,2,0:T(2,128)} %copy.67), calls=%async_computation.1 | async-start | bytes 262144 | tf_op jit(solution)/shard_map/all_to_all | solution.py:110
  34.1 1.1 copy.64
  35.2 1.1 pad_maximum_fusion
  36.3 2.0 gather_fusion
  38.3 13.3 %all-to-all-done.1 = f32[128,2,2]{1,2,0:T(2,128)S(1)} async-done(((f32[128,2,2]{1,2,0:T(2,128)}), f32[128,2,2]{1,2,0:T(2,128)S(1)}, u32[]{:S(2)}, u32[]{:S(2)}) %all-to-all-start.1) | async-done | bytes 2080 | tf_op jit(solution)/shard_map/all_to_all | solution.py:110
  51.5 6.9 %all-to-all-start = ((f32[256,5,128]{2,1,0:T(8,128)}), f32[256,5,128]{2,1,0:T(8,128)S(1)}, u32[]{:S(2)}, u32[]{:S(2)}) async-start(f32[256,5,128]{2,1,0:T(8,128)} %gather_fusion), calls=%async_computation | async-start | bytes 2097152 | tf_op jit(solution)/shard_map/all_to_all | solution.py:109
  58.5 3.0 gather_fusion.3
  61.5 51.4 %all-to-all-done = f32[256,5,128]{2,1,0:T(8,128)S(1)} async-done(((f32[256,5,128]{2,1,0:T(8,128)}), f32[256,5,128]{2,1,0:T(8,128)S(1)}, u32[]{:S(2)}, u32[]{:S(2)}) %all-to-all-start) | async-done | bytes 655392 | tf_op jit(solution)/shard_map/all_to_all | solution.py:109
  112.9 1.0 copy-done.2
  114.0 8.9 %all-to-all-start.2 = ((bf16[256,64,128]{2,1,0:T(8,128)(2,1)}), bf16[256,64,128]{2,1,0:T(8,128)(2,1)}, u32[]{:S(2)}, u32[]{:S(2)}) async-start(bf16[256,64,128]{2,1,0:T(8,128)(2,1)} %gather_fusion.3), calls=%async_computation.2 | async-start | bytes 8388608 | tf_op jit(solution)/shard_map/all_to_all | solution.py:105
  123.1 1.2 gather_fusion.2
  124.6 1.3 slice.46
  125.9 1.9 fusion.15
  127.8 180.4 %all-to-all-done.2 = bf16[256,64,128]{2,1,0:T(8,128)(2,1)} async-done(((bf16[256,64,128]{2,1,0:T(8,128)(2,1)}), bf16[256,64,128]{2,1,0:T(8,128)(2,1)}, u32[]{:S(2)}, u32[]{:S(2)}) %all-to-all-start.2) | async-done | bytes 4194336 | tf_op jit(solution)/shard_map/all_to_all | solution.py:105
  308.2 3.4 fusion.16
  312.1 1.1 copy.73
  313.2 12.1 %all-to-all-start.3 = ((f32[256,4,128]{2,1,0:T(4,128)}), f32[256,4,128]{2,1,0:T(4,128)S(1)}, u32[]{:S(2)}, u32[]{:S(2)}) async-start(f32[256,4,128]{2,1,0:T(4,128)} %copy.73), calls=%async_computation.3 | async-start | bytes 1048576 | tf_op jit(solution)/shard_map/all_to_all | solution.py:122
  325.5 4.5 %convolution_multiply_fusion = f32[256,4,64]{2,1,0:T(4,128)S(1)} fusion(bf16[256,64,128]{2,1,0:T(8,128)(2,1)} %all-to-all-done.2, bf16[256,4,128]{2,0,1:T(8,128)(2,1)S(1)} %pad_maximum_fusion.2), kind=kOutput, calls=%fused_computation.6 | convolution fusion | flops 16842752 | bytes 4718592 | tf_op jit(solution)/shard_map/ncp,nkp->nck/dot_general | solution.py:44
  330.2 1.0 fusion.2
  331.2 27.3 %all-to-all-done.3 = f32[256,4,128]{2,1,0:T(4,128)S(1)} async-done(((f32[256,4,128]{2,1,0:T(4,128)}), f32[256,4,128]{2,1,0:T(4,128)S(1)}, u32[]{:S(2)}, u32[]{:S(2)}) %all-to-all-start.3) | async-done | bytes 524320 | tf_op jit(solution)/shard_map/all_to_all | solution.py:122
  359.4 1.1 slice_select_fusion
  (42 shorter events, 5.2 us)
Async XLA Ops:
  7.2 51.3 %copy-start = (bf16[128,64,128]{2,1,0:T(8,128)(2,1)S(1)}, bf16[128,64,128]{2,1,0:T(8,128)(2,1)}, u32[]{:S(2)}) copy-start(bf16[128,64,128]{2,1,0:T(8,128)(2,1)} %param.11) | copy-start | bytes 6291460
  13.6 38.0 %all-to-all-start.1 = ((f32[128,2,2]{1,2,0:T(2,128)}), f32[128,2,2]{1,2,0:T(2,128)S(1)}, u32[]{:S(2)}, u32[]{:S(2)}) async-start(f32[128,2,2]{1,2,0:T(2,128)} %copy.67), calls=%async_computation.1 | async-start | bytes 262144 | tf_op jit(solution)/shard_map/all_to_all | solution.py:110
  51.5 61.4 %all-to-all-start = ((f32[256,5,128]{2,1,0:T(8,128)}), f32[256,5,128]{2,1,0:T(8,128)S(1)}, u32[]{:S(2)}, u32[]{:S(2)}) async-start(f32[256,5,128]{2,1,0:T(8,128)} %gather_fusion), calls=%async_computation | async-start | bytes 2097152 | tf_op jit(solution)/shard_map/all_to_all | solution.py:109
  61.5 61.6 %copy-start.1 = (bf16[256,256]{1,0:T(8,128)(2,1)S(1)}, bf16[256,256]{1,0:T(8,128)(2,1)}, u32[]{:S(2)}) copy-start(bf16[256,256]{1,0:T(8,128)(2,1)} %param.15) | copy-start | bytes 393220
  112.9 1.0 copy-start.2
  114.0 194.2 %all-to-all-start.2 = ((bf16[256,64,128]{2,1,0:T(8,128)(2,1)}), bf16[256,64,128]{2,1,0:T(8,128)(2,1)}, u32[]{:S(2)}, u32[]{:S(2)}) async-start(bf16[256,64,128]{2,1,0:T(8,128)(2,1)} %gather_fusion.3), calls=%async_computation.2 | async-start | bytes 8388608 | tf_op jit(solution)/shard_map/all_to_all | solution.py:105
  313.2 45.3 %all-to-all-start.3 = ((f32[256,4,128]{2,1,0:T(4,128)}), f32[256,4,128]{2,1,0:T(4,128)S(1)}, u32[]{:S(2)}, u32[]{:S(2)}) async-start(f32[256,4,128]{2,1,0:T(4,128)} %copy.73), calls=%async_computation.3 | async-start | bytes 1048576 | tf_op jit(solution)/shard_map/all_to_all | solution.py:122
  325.3 36.6 %reduce-scatter.2.cloned.1.call-start = ((), (), s32[]{:S(2)}) async-start(), calls=%async_computation.5 | async-start | bytes 327680 | tf_op jit(solution)/shard_map/reduce_scatter | solution.py:134
  325.4 35.8 %copy-start.3 = (f32[128,128]{1,0:T(8,128)S(1)}, f32[128,128]{1,0:T(8,128)}, u32[]{:S(2)}) copy-start(f32[128,128]{1,0:T(8,128)} %param.10) | copy-start | bytes 196612
Sparse Core Ops, SparseCore 0:
  331.3 27.4 reduce-scatter.1
where the time goes:
time: 369 us
  waiting for transfers between devices  272 us (74%)
  starting transfers between devices  48.6 us (13%)
  local copies, waits for them, and re-layouts  18.7 us (5%)
  between operations  15.1 us (4%)
  matrix products  8.87 us (2%)
  other arithmetic  5.07 us (1%)
    all_to_all x1, waiting for transfers between devices, per_device(): lax.all_to_all(sent_tiles, 'cells', split_axis=0, concat_axis=0, tiled=True)  180 us
    all_to_all x1, waiting for transfers between devices, per_device(): lax.all_to_all(spray_condition, 'cells', split_axis=0, concat_axis=0, til...  51.4 us
    all_to_all x1, waiting for transfers between devices, per_device(): lax.all_to_all(jnp.concatenate([relocated_bundles, particles_after_heatin...  27.3 us
    all_to_all x1, starting transfers between devices, per_device(): lax.all_to_all(labels, 'cells', split_axis=0, concat_axis=0, tiled=True)  20.6 us
    all_to_all x1, waiting for transfers between devices, per_device(): lax.all_to_all(labels, 'cells', split_axis=0, concat_axis=0, tiled=True)  13.3 us
    all_to_all x1, starting transfers between devices, per_device(): lax.all_to_all(jnp.concatenate([relocated_bundles, particles_after_heatin...  12.1 us
    all_to_all x1, starting transfers between devices, per_device(): lax.all_to_all(sent_tiles, 'cells', split_axis=0, concat_axis=0, tiled=True)  8.94 us
  transfers between devices with their start and end apart: 5, of which 4 were waited for; matrix products, arithmetic and copies ran while one was open for 6% of the time, Pallas kernels for 0%

commit v1 on v0

v1 whole, which is shorter than its diff:
```python
import functools

import jax
import jax.numpy as jnp
from jax import lax
from jax.experimental import pallas as pl
from jax.experimental.pallas import tpu as pltpu
from jax.sharding import PartitionSpec as P

MESH = pl.DeviceIdType.MESH
F32, BF16, I32 = jnp.float32, jnp.bfloat16, jnp.int32

REYNOLDS_SCALE = 20.0
DRAG_SCALE = 1.0
HEAT_SCALE = 0.5
PRANDTL_ROOT = 0.9
LOADING = 0.2
ABSENT = 1.0e9


def iota(shape, axis):
    return lax.broadcasted_iota(I32, shape, axis)


def to_row(column):
    n = column.shape[0]
    eye = iota((n, n), 0) == iota((n, n), 1)
    return jnp.sum(jnp.where(eye, column, 0.0), axis=0, keepdims=True)


def to_column(row):
    n = row.shape[1]
    eye = iota((n, n), 0) == iota((n, n), 1)
    return jnp.sum(jnp.where(eye, row, 0.0), axis=1, keepdims=True)


def halves(x):
    high = x.astype(BF16)
    return high, (x - high.astype(F32)).astype(BF16)


def dot(a, b):
    return jnp.dot(a, b, preferred_element_type=F32)


def step_kernel(
    nz,
    ncore,
    na,
    nrep,
    owner_ref,
    place_ref,
    busy_ref,
    field_ref,
    tiles_hbm,
    speed_hbm,
    size_hbm,
    heat_hbm,
    moved_hbm,
    warmed_hbm,
    source_ref,
    tiles,
    speed,
    size,
    heat,
    moved,
    warmed,
    lab_a,
    lab_z,
    row_zs,
    row_zr,
    row_as,
    row_ar,
    sums_as,
    sums_ar,
    sums_zs,
    sums_zr,
    part_s,
    part_r,
    in_sem,
    out_sem,
    send_sem,
    recv_sem,
):
    blocks = tiles.shape[0]
    cells = tiles.shape[1]
    width = 4 * cells
    owned = field_ref.shape[0]
    sources = nz * na
    slots = 2 * sources
    me = lax.axis_index("cells")
    r = lax.axis_index("rep")
    core = lax.rem(me, ncore)
    z = lax.rem(me // ncore, nz)
    y = me // (ncore * nz)
    a = y * ncore + core

    def at_z(step):
        other = lax.rem(z + step, nz)
        return other, {"cells": (y * nz + other) * ncore + core, "rep": r}

    def at_a(step):
        other = lax.rem(a + step, na)
        return other, {
            "cells": ((other // ncore) * nz + z) * ncore + lax.rem(other, ncore),
            "rep": r,
        }

    def at_r(step):
        other = lax.rem(r + step, nrep)
        return other, {"cells": me, "rep": other}

    inputs = [
        pltpu.make_async_copy(src, dst, in_sem.at[i])
        for i, (src, dst) in enumerate(
            ((tiles_hbm, tiles), (speed_hbm, speed), (size_hbm, size), (heat_hbm, heat))
        )
    ]
    for copy in inputs:
        copy.start()

    barrier = pltpu.get_barrier_semaphore()
    for where, count in ((at_z, nz), (at_a, na), (at_r, nrep)):
        for step in range(1, count):
            pl.semaphore_signal(
                barrier, inc=1, device_id=where(step)[1], device_id_type=MESH
            )
    pl.semaphore_wait(barrier, nz + na + nrep - 3)

    def exchange(phase, where, count, source, target, mine):
        for step in range(1, count):
            other, device = where(step)
            pltpu.make_async_remote_copy(
                src_ref=source(other),
                dst_ref=target.at[mine],
                send_sem=send_sem.at[phase],
                recv_sem=recv_sem.at[phase],
                device_id=device,
                device_id_type=MESH,
            ).start()

    def arrived(phase, where, count, target):
        some = target.at[pl.ds(0, count - 1)]
        pltpu.make_async_remote_copy(
            src_ref=some,
            dst_ref=some,
            send_sem=send_sem.at[phase],
            recv_sem=recv_sem.at[phase],
            device_id=where(1)[1],
            device_id_type=MESH,
        ).wait()

    owner = owner_ref[...]
    live = iota((1, blocks), 1) < busy_ref[0]
    label = jnp.where(live, owner * owned + place_ref[...], -1)
    lab_a[a] = label
    exchange(0, at_a, na, lambda other: lab_a.at[a], lab_a, a)

    ownerf = owner.astype(F32)
    earlier = (
        (to_column(ownerf) == ownerf)
        & (iota((blocks, blocks), 0) < iota((blocks, blocks), 1))
        & (iota((blocks, blocks), 0) < busy_ref[0])
    )
    rank = jnp.sum(jnp.where(earlier, 1.0, 0.0), axis=0, keepdims=True).astype(I32)
    owner_y = owner // (nz * ncore)
    owner_rest = owner - owner_y * (nz * ncore)
    owner_z = owner_rest // ncore
    owner_a = owner_y * ncore + (owner_rest - owner_z * ncore)
    slot = jnp.where(live, owner_a * (2 * nz) + rank * nz + owner_z, -1)
    slot_column = to_column(slot.astype(F32))
    to_slots = jnp.where(iota((slots, blocks), 0) == slot, 1.0, 0.0).astype(BF16)
    from_slots = jnp.where(
        iota((blocks, slots), 1).astype(F32) == slot_column, 1.0, 0.0
    ).astype(BF16)

    arrived(0, at_a, na, lab_a)
    lab_z[z] = lab_a[...].reshape(na, blocks)
    exchange(1, at_z, nz, lambda other: lab_z.at[z], lab_z, z)
    arrived(1, at_z, nz, lab_z)

    place = lab_z[...].reshape(sources, blocks) - me * owned
    match = (place >= 0) & (place < owned)
    key = (iota((sources, blocks), 1) * owned + place).astype(F32)
    first = jnp.min(jnp.where(match, key, ABSENT), axis=1, keepdims=True)
    last = jnp.max(jnp.where(match, key, -1.0), axis=1, keepdims=True)
    size_f = float(owned)
    place_0 = jnp.where(first < ABSENT, first - jnp.floor(first / size_f) * size_f, -1.0)
    place_1 = jnp.where(last > first, last - jnp.floor(last / size_f) * size_f, -1.0)
    lanes = iota((sources, owned), 1).astype(F32)
    field = field_ref[...]
    rows = [
        dot(jnp.where(lanes == p, 1.0, 0.0).astype(BF16), field).reshape(nz, na, width)
        for p in (place_0, place_1)
    ]
    row_zs[...] = jnp.concatenate(rows, axis=1).astype(BF16)
    exchange(2, at_z, nz, lambda other: row_zs.at[other], row_zr, z)
    row_zr[z] = row_zs[z]
    deposits = [
        jnp.where(
            iota((owned, sources), 0).astype(F32) == to_row(p), 1.0, 0.0
        ).astype(BF16)
        for p in (place_0, place_1)
    ]

    out_row, in_row = iota((slots, slots), 0), iota((slots, slots), 1)
    out_a = out_row // (2 * nz)
    out_rest = out_row - out_a * (2 * nz)
    out_rank = out_rest // nz
    out_z = out_rest - out_rank * nz
    regroup = jnp.where(
        in_row == out_z * (2 * na) + out_rank * na + out_a, 1.0, 0.0
    ).astype(BF16)
    arrived(2, at_z, nz, row_zr)
    row_as[...] = (
        dot(regroup, row_zr[...].reshape(slots, width))
        .astype(BF16)
        .reshape(na, 2 * nz, width)
    )
    exchange(3, at_a, na, lambda other: row_as.at[other], row_ar, a)
    row_ar[a] = row_as[a]
    spread_in, spread_out = iota((width, 8 * cells), 0), iota((width, 8 * cells), 1)
    out_c = spread_out // (2 * cells)
    out_k = spread_out - (spread_out // cells) * cells
    spread = jnp.where(spread_in == out_c * cells + out_k, 1.0, 0.0).astype(BF16)
    arrived(3, at_a, na, row_ar)

    gas = dot(from_slots, row_ar[...].reshape(slots, width)).astype(BF16)
    gas = dot(gas, spread)
    for copy in inputs:
        copy.wait()
    diagonal = iota((8, 8 * cells), 1) // cells == iota((8, 8 * cells), 0)
    pair = 2 * cells
    sampled = []
    for g in range(blocks // 8):
        left = []
        for c in range(4):
            piece = gas[8 * g : 8 * g + 8, c * pair : (c + 1) * pair]
            left.append(
                jnp.where(diagonal, jnp.concatenate([piece] * 4, axis=1), 0.0)
            )
        left = jnp.concatenate(left, axis=0).astype(BF16)
        sampled.append(
            dot(left, tiles[8 * g : 8 * g + 8].reshape(8 * cells, tiles.shape[2]))
        )
    scale = 2.0 / cells
    u = [
        jnp.concatenate([s[8 * c : 8 * c + 8] for s in sampled], axis=0) * scale
        for c in range(4)
    ]

    v = [speed[c] for c in range(3)]
    d = size[...]
    t = heat[...]
    slip = [u[c] - v[c] for c in range(3)]
    slip_speed = jnp.sqrt(
        1.0 + (slip[0] * slip[0] + slip[1] * slip[1] + slip[2] * slip[2])
    )
    reynolds = REYNOLDS_SCALE * d * slip_speed
    squared = d * d
    drag = DRAG_SCALE * (1.0 + 0.15 * jnp.exp(0.687 * jnp.log(reynolds))) / squared
    warm = HEAT_SCALE * (2.0 + 0.6 * PRANDTL_ROOT * jnp.sqrt(reynolds)) / squared
    mass = LOADING * d * squared
    live_column = slot_column >= 0.0
    terms = []
    for c in range(3):
        new = (v[c] + drag * u[c]) / (1.0 + drag)
        terms.append((-mass * (new - v[c])).astype(BF16))
        moved[c] = jnp.where(live_column, new, v[c])
    new = (t + warm * u[3]) / (1.0 + warm)
    terms.append((-mass * (new - t)).astype(BF16))
    warmed[...] = jnp.where(live_column, new, t)
    outputs = [
        pltpu.make_async_copy(src, dst, out_sem.at[i])
        for i, (src, dst) in enumerate(((moved, moved_hbm), (warmed, warmed_hbm)))
    ]
    for copy in outputs:
        copy.start()

    lane, line = iota((32, pair), 1), iota((32, pair), 0)
    line = line - (line // 8) * 8
    low = iota((8, pair), 1) < cells
    rows = []
    termf = [x.astype(F32) for x in terms]
    for g in range(blocks // 8):
        left = jnp.concatenate([x[8 * g : 8 * g + 8] for x in termf], axis=0)
        full = lax.dot_general(
            left.astype(BF16),
            tiles[8 * g : 8 * g + 8].reshape(8 * cells, tiles.shape[2]),
            (((1,), (1,)), ((), ())),
            preferred_element_type=F32,
        )
        own = jnp.zeros((32, pair), F32)
        for j in range(4):
            keep = line == 2 * j + lane // cells
            own = own + jnp.where(keep, full[:, j * pair : (j + 1) * pair], 0.0)
        own = own + pltpu.roll(own, cells, axis=1)
        rows.append(
            jnp.concatenate(
                [
                    jnp.where(low, own[0:8], own[8:16]),
                    jnp.where(low, own[16:24], own[24:32]),
                ],
                axis=1,
            )
        )
    high, rest = halves(jnp.concatenate(rows, axis=0) * scale)
    slotted = (dot(to_slots, high) + dot(to_slots, rest)).reshape(na, 2 * nz, width)
    group = 4 * nz
    sums_as[...] = jnp.concatenate(
        [slotted[..., :128], slotted[..., 128:]], axis=1
    ).reshape(na * group, 128)

    def of_group(ref, other):
        return ref.at[pl.ds(pl.multiple_of(other * group, group), group)]

    for step in range(1, na):
        other, device = at_a(step)
        pltpu.make_async_remote_copy(
            src_ref=of_group(sums_as, other),
            dst_ref=of_group(sums_ar, a),
            send_sem=send_sem.at[4],
            recv_sem=recv_sem.at[4],
            device_id=device,
            device_id_type=MESH,
        ).start()
    mine = pl.ds(pl.multiple_of(a * group, group), group)
    sums_ar[mine, :] = sums_as[mine, :]
    some = sums_ar.at[pl.ds(0, (na - 1) * group)]
    pltpu.make_async_remote_copy(
        src_ref=some,
        dst_ref=some,
        send_sem=send_sem.at[4],
        recv_sem=recv_sem.at[4],
        device_id=at_a(1)[1],
        device_id_type=MESH,
    ).wait()
    for other in range(nz):
        for k in range(2):
            for half in range(2):
                sums_zs[other, pl.ds(k * na, na), pl.ds(128 * half, 128)] = sums_ar[
                    pl.ds((2 * half + k) * nz + other, na, stride=group), :
                ]
    exchange(5, at_z, nz, lambda other: sums_zs.at[other], sums_zr, z)
    sums_zr[z] = sums_zs[z]
    arrived(5, at_z, nz, sums_zr)

    total = jnp.zeros((owned, width), F32)
    for k in range(2):
        got = sums_zr[:, k * na : (k + 1) * na, :].reshape(sources, width)
        high, rest = halves(got)
        total = total + dot(deposits[k], high) + dot(deposits[k], rest)
    part_s[...] = total.reshape(nrep, owned // nrep, width)
    exchange(6, at_r, nrep, lambda other: part_s.at[other], part_r, r)
    part_r[r] = part_s[r]
    arrived(6, at_r, nrep, part_r)
    total = part_r[0]
    for k in range(1, nrep):
        total = total + part_r[k]
    source_ref[...] = total
    for copy in outputs:
        copy.wait()


def per_device(
    ny,
    nz,
    ncore,
    nrep,
    particle_speeds,
    particle_diameters,
    particle_kelvins,
    unscaled_kernel_coefficients,
    bundle_patch_ordinal,
    bundle_patch_custodian,
    busy_bundles_per_accelerator,
    ambient_flow_quantities,
):
    blocks, cells, parcels = unscaled_kernel_coefficients.shape
    owned, width = ambient_flow_quantities.shape
    na = ny * ncore
    sources = na * nz
    slots = 2 * sources
    anywhere = pl.BlockSpec(memory_space=pl.ANY)
    vmem = pl.BlockSpec(memory_space=pltpu.VMEM)
    smem = pl.BlockSpec(memory_space=pltpu.SMEM)
    moved, warmed, source = pl.pallas_call(
        functools.partial(step_kernel, nz, ncore, na, nrep),
        out_shape=(
            jax.ShapeDtypeStruct((3, blocks, parcels), F32),
            jax.ShapeDtypeStruct((blocks, parcels), F32),
            jax.ShapeDtypeStruct((owned // nrep, width), F32),
        ),
        in_specs=[vmem, vmem, smem, vmem] + [anywhere] * 4,
        out_specs=(anywhere, anywhere, vmem),
        scratch_shapes=[
            pltpu.VMEM((blocks, cells, parcels), BF16),
            pltpu.VMEM((3, blocks, parcels), F32),
            pltpu.VMEM((blocks, parcels), F32),
            pltpu.VMEM((blocks, parcels), F32),
            pltpu.VMEM((3, blocks, parcels), F32),
            pltpu.VMEM((blocks, parcels), F32),
            pltpu.VMEM((na, 1, blocks), I32),
            pltpu.VMEM((nz, na, blocks), I32),
            pltpu.VMEM((nz, 2 * na, width), BF16),
            pltpu.VMEM((nz, 2 * na, width), BF16),
            pltpu.VMEM((na, 2 * nz, width), BF16),
            pltpu.VMEM((na, 2 * nz, width), BF16),
            pltpu.VMEM((2 * slots, width // 2), F32),
            pltpu.VMEM((2 * slots, width // 2), F32),
            pltpu.VMEM((nz, 2 * na, width), F32),
            pltpu.VMEM((nz, 2 * na, width), F32),
            pltpu.VMEM((nrep, owned // nrep, width), F32),
            pltpu.VMEM((nrep, owned // nrep, width), F32),
            pltpu.SemaphoreType.DMA((4,)),
            pltpu.SemaphoreType.DMA((2,)),
            pltpu.SemaphoreType.DMA((7,)),
            pltpu.SemaphoreType.DMA((7,)),
        ],
        compiler_params=pltpu.CompilerParams(
            collective_id=0, has_side_effects=True, vmem_limit_bytes=40 * 2**20
        ),
        name="parcel_step",
    )(
        bundle_patch_custodian.reshape(1, blocks),
        bundle_patch_ordinal.reshape(1, blocks),
        busy_bundles_per_accelerator,
        ambient_flow_quantities,
        unscaled_kernel_coefficients,
        jnp.transpose(particle_speeds, (1, 0, 2)),
        particle_diameters,
        particle_kelvins,
    )
    return jnp.transpose(moved, (1, 0, 2)), warmed, source


def solution(mesh, ny=4, nz=16, ncore=2):
    both = ("cells", "rep")
    return jax.shard_map(
        functools.partial(per_device, ny, nz, ncore, mesh.shape["rep"]),
        mesh=mesh,
        in_specs=(
            P(both, None, None),
            P(both, None),
            P(both, None),
            P(both, None, None),
            P(both),
            P(both),
            P(both),
            P("cells", None),
        ),
        out_specs=(P(both, None, None), P(both, None), P(both, None)),
        check_vma=False,
    )
```

time: 369 us -> 78.9 us (0.21)
  waiting for transfers between devices: 272 us -> 0 us
  Pallas kernels: 0 us -> 67.9 us
  starting transfers between devices: 48.6 us -> 0 us
  between operations: 15.1 us -> 1.3 us
  local copies, waits for them, and re-layouts: 18.7 us -> 8.34 us
  matrix products: 8.87 us -> 0 us
  other arithmetic: 5.07 us -> 0 us
    all_to_all x4 -> x0, waiting for transfers between devices: 272 us -> none  [the longest x1 180 us: per_device(): lax.all_to_all(sent_tiles, 'cells', split_axis=0, concat_axis=0, tiled=True)]
    pallas_call x0 -> x1, Pallas kernels: none -> 67.9 us  [per_device(): pl.pallas_call(functools.partial(step_kernel, nz, ncore, na, nrep), out_s...]
    all_to_all x4 -> x0, starting transfers between devices: 48.6 us -> none  [the longest x1 20.6 us: per_device(): lax.all_to_all(labels, 'cells', split_axis=0, concat_axis=0, tiled=True)]
    gather x6 -> x0, local copies, waits for them, and re-layouts: 8.92 us -> none  [the longest x1 3.03 us: per_device(): sent_tiles = unscaled_kernel_coefficients[picked]]
    dot_general x3 -> x0, matrix products: 8.87 us -> none  [the longest x1 4.48 us: integrate_timestep(): jnp.einsum('ncp,nkp->nck', rounded, tiles_here, preferred_element_type=jn...]
    unnamed x10 -> x17, local copies, waits for them, and re-layouts: 2.81 us -> 8.34 us
  transfers between devices with their start and end apart: 5 -> 0, of which waited for: 4 -> 0; matrix products, arithmetic and copies ran while one was open for 6% -> 0% of each run, Pallas kernels for 0% -> 0%
where the time goes in v1:
time: 78.9 us; the launch traced here: 77.5 us
  Pallas kernels  67.9 us (86%)
  local copies, waits for them, and re-layouts  8.34 us (11%)
  between operations  1.3 us (2%)
    pallas_call x1, Pallas kernels, per_device(): pl.pallas_call(functools.partial(step_kernel, nz, ncore, na, nrep), out_s...  67.9 us
    unnamed x17, local copies, waits for them, and re-layouts  8.34 us

profile of v1, /device:TPU:1, one launch (start us, length us, event | category | flops | bytes accessed | tf_op | source)
XLA Modules:
  0.0 77.5 jit_solution(14617019331646215882)
XLA Ops:
  1.3 0.0 copy-start
  1.3 1.6 %copy-done = bf16[128,64,128]{2,1,0:T(8,128)(2,1)S(1)} copy-done((bf16[128,64,128]{2,1,0:T(8,128)(2,1)S(1)}, bf16[128,64,128]{2,1,0:T(8,128)(2,1)}, u32[]{:S(2)}) %copy-start) | copy-done | bytes 2097176
  2.9 0.0 copy-start.1
  2.9 0.9 %copy-done.1 = f32[128,3,128]{2,0,1:T(8,128)S(1)} copy-done((f32[128,3,128]{2,0,1:T(8,128)S(1)}, f32[128,3,128]{2,0,1:T(8,128)}, u32[]{:S(2)}) %copy-start.1) | copy-done | bytes 196632
  3.8 0.0 copy-start.2
  3.8 0.9 %copy-done.2 = bf16[256,256]{1,0:T(8,128)(2,1)S(1)} copy-done((bf16[256,256]{1,0:T(8,128)(2,1)S(1)}, bf16[256,256]{1,0:T(8,128)(2,1)}, u32[]{:S(2)}) %copy-start.2) | copy-done | bytes 131096
  4.7 0.0 copy-start.3
  4.7 0.8 %copy-done.3 = f32[128,128]{1,0:T(8,128)S(1)} copy-done((f32[128,128]{1,0:T(8,128)S(1)}, f32[128,128]{1,0:T(8,128)}, u32[]{:S(2)}) %copy-start.3) | copy-done | bytes 65560
  5.5 0.0 copy-start.4
  5.5 0.8 %copy-done.4 = f32[128,128]{1,0:T(8,128)S(1)} copy-done((f32[128,128]{1,0:T(8,128)S(1)}, f32[128,128]{1,0:T(8,128)}, u32[]{:S(2)}) %copy-start.4) | copy-done | bytes 65560
  6.4 0.0 copy-start.5
  6.4 0.7 copy-done.5
  7.0 0.0 copy-start.6
  7.0 0.7 copy-done.6
  7.7 67.9 %parcel_step.1 = (f32[3,128,128]{2,1,0:T(8,128)S(1)}, f32[128,128]{1,0:T(8,128)S(1)}, f32[64,256]{1,0:T(8,128)S(1)}) custom-call(s32[1,128]{1,0:T(1,128)S(1)} %bitcast.6, s32[1,128]{1,0:T(1,128)S(1)} %bitcast.7, s32[1]{0:T(128)S(6)} %copy.14.busy_ref, bf16[256,256]{1,0:T(8,128)(2,1)S(1)} %copy-done.2, bf16[128,64,128]{2,1,0:T(8,128)(2,1)S(1)} %copy-done, ...), custom_call_target="tpu_custom_call" | custom-call | tf_op jit(solution)/shard_map/parcel_step/pallas_call | solution.py:387
  75.6 0.7 copy.15
  76.2 0.6 copy.16
  76.9 0.6 copy.17
Async XLA Ops:
  1.3 1.6 %copy-start = (bf16[128,64,128]{2,1,0:T(8,128)(2,1)S(1)}, bf16[128,64,128]{2,1,0:T(8,128)(2,1)}, u32[]{:S(2)}) copy-start(bf16[128,64,128]{2,1,0:T(8,128)(2,1)} %tiles_hbm.1) | copy-start | bytes 6291460
  2.9 0.9 %copy-start.1 = (f32[128,3,128]{2,0,1:T(8,128)S(1)}, f32[128,3,128]{2,0,1:T(8,128)}, u32[]{:S(2)}) copy-start(f32[128,3,128]{2,0,1:T(8,128)} %param.8) | copy-start | bytes 589828
  3.8 0.9 %copy-start.2 = (bf16[256,256]{1,0:T(8,128)(2,1)S(1)}, bf16[256,256]{1,0:T(8,128)(2,1)}, u32[]{:S(2)}) copy-start(bf16[256,256]{1,0:T(8,128)(2,1)} %field_ref.1) | copy-start | bytes 393220
  4.7 0.8 %copy-start.3 = (f32[128,128]{1,0:T(8,128)S(1)}, f32[128,128]{1,0:T(8,128)}, u32[]{:S(2)}) copy-start(f32[128,128]{1,0:T(8,128)} %size_hbm.1) | copy-start | bytes 196612
  5.5 0.8 %copy-start.4 = (f32[128,128]{1,0:T(8,128)S(1)}, f32[128,128]{1,0:T(8,128)}, u32[]{:S(2)}) copy-start(f32[128,128]{1,0:T(8,128)} %heat_hbm.1) | copy-start | bytes 196612
  6.4 0.7 copy-start.5
  7.0 0.7 copy-start.6

commit v2 on v1

v2 whole, which is shorter than its diff:
```python
import functools

import jax
import jax.numpy as jnp
from jax import lax
from jax.experimental import pallas as pl
from jax.experimental.pallas import tpu as pltpu
from jax.sharding import PartitionSpec as P

MESH = pl.DeviceIdType.MESH
F32, BF16, I32 = jnp.float32, jnp.bfloat16, jnp.int32

REYNOLDS_SCALE = 20.0
DRAG_SCALE = 1.0
HEAT_SCALE = 0.5
PRANDTL_ROOT = 0.9
LOADING = 0.2
ABSENT = 1.0e9


def iota(shape, axis):
    return lax.broadcasted_iota(I32, shape, axis)


def to_row(column):
    n = column.shape[0]
    eye = iota((n, n), 0) == iota((n, n), 1)
    return jnp.sum(jnp.where(eye, column, 0.0), axis=0, keepdims=True)


def to_column(row):
    n = row.shape[1]
    eye = iota((n, n), 0) == iota((n, n), 1)
    return jnp.sum(jnp.where(eye, row, 0.0), axis=1, keepdims=True)


def halves(x):
    high = x.astype(BF16)
    return high, (x - high.astype(F32)).astype(BF16)


def dot(a, b):
    return jnp.dot(a, b, preferred_element_type=F32)


def step_kernel(
    ny,
    nz,
    nrep,
    owner_hbm,
    place_hbm,
    busy_ref,
    field_hbm,
    tiles_hbm,
    speed_hbm,
    size_hbm,
    heat_hbm,
    moved_hbm,
    warmed_hbm,
    source_ref,
    owner_v,
    place_v,
    field_v,
    tiles,
    speed,
    size,
    heat,
    moved,
    warmed,
    lab_mine,
    lab_other,
    lab_all,
    row_s,
    row_r,
    row_x,
    sums_x,
    sums_s,
    sums_r,
    part_s,
    part_r,
    in_sem,
    out_sem,
    send_sem,
    recv_sem,
):
    blocks, cells, parcels = tiles.shape
    width = 4 * cells
    owned = field_v.shape[0]
    chips = ny * nz
    sources = 2 * chips
    slots = 2 * sources
    me = lax.axis_index("cells")
    r = lax.axis_index("rep")
    core = me & 1
    chip = me >> 1
    z = chip & (nz - 1)
    y = chip // nz
    steps = sorted(
        ((dy, dz) for dy in range(ny) for dz in range(nz) if dy or dz),
        key=lambda step: (
            -min(step[0], ny - step[0]) - min(step[1], nz - step[1]),
            step,
        ),
    )
    others = []
    for dy, dz in steps:
        other = ((y + dy) & (ny - 1)) * nz + ((z + dz) & (nz - 1))
        others.append((other, {"cells": other * 2 + core, "rep": r}))
    sibling = {"cells": chip * 2 + (1 - core), "rep": r}
    reps = []
    for step in range(1, nrep):
        other = (r + step) & (nrep - 1)
        reps.append((other, {"cells": me, "rep": other}))

    inputs = [
        pltpu.make_async_copy(src, dst, in_sem.at[i])
        for i, (src, dst) in enumerate(
            (
                (owner_hbm, owner_v),
                (place_hbm, place_v),
                (field_hbm, field_v),
                (tiles_hbm, tiles),
                (speed_hbm, speed),
                (size_hbm, size),
                (heat_hbm, heat),
            )
        )
    ]
    for copy in inputs:
        copy.start()

    barrier = pltpu.get_barrier_semaphore()
    for device in [device for _, device in others + reps] + [sibling]:
        pl.semaphore_signal(barrier, inc=1, device_id=device, device_id_type=MESH)

    def send(phase, src, dst, device):
        copy = pltpu.make_async_remote_copy(
            src_ref=src,
            dst_ref=dst,
            send_sem=send_sem.at[phase],
            recv_sem=recv_sem.at[phase],
            device_id=device,
            device_id_type=MESH,
        )
        copy.start()
        return copy

    def arrived(phase, some):
        pltpu.make_async_remote_copy(
            src_ref=some,
            dst_ref=some,
            send_sem=send_sem.at[phase],
            recv_sem=recv_sem.at[phase],
            device_id=sibling,
            device_id_type=MESH,
        ).wait()

    target = iota((1, 8 * cells), 1)
    target = (target // (2 * cells)) * cells + (target & (cells - 1))
    spread = jnp.where(iota((width, 8 * cells), 0) == target, 1.0, 0.0).astype(BF16)
    diagonal = (iota((1, 8 * cells), 1) // cells) == iota((8, 1), 0)
    slot_line = iota((slots, 1), 0)
    slot_rank = slot_line & 1
    slot_source = ((slot_line & (sources - 1)) >> 1) * 2 + slot_line // sources

    inputs[0].wait()
    inputs[1].wait()
    owner = owner_v[...]
    live = iota((1, blocks), 1) < busy_ref[0]
    label = jnp.where(live, owner * owned + place_v[...], -1)
    lab_mine[...] = label

    ownerf = owner.astype(F32)
    earlier = (
        (to_column(ownerf) == ownerf)
        & (iota((blocks, blocks), 0) < iota((blocks, blocks), 1))
        & (iota((blocks, blocks), 0) < busy_ref[0])
    )
    rank = jnp.sum(jnp.where(earlier, 1.0, 0.0), axis=0, keepdims=True).astype(I32)
    slot = jnp.where((owner & 1) == core, 0, sources) + (owner >> 1) * 2 + rank
    slot = jnp.where(live, slot, -1)
    slot_column = to_column(slot.astype(F32))
    to_slots = jnp.where(slot_line == slot, 1.0, 0.0).astype(BF16)
    from_slots = jnp.where(
        iota((1, slots), 1).astype(F32) == slot_column, 1.0, 0.0
    ).astype(BF16)

    pl.semaphore_wait(barrier, chips - 1 + nrep - 1 + 1)

    send(0, lab_mine, lab_other, sibling).wait()
    got = lab_other[...]
    lab_all[chip] = jnp.concatenate(
        [jnp.where(core == 0, label, got), jnp.where(core == 0, got, label)], axis=0
    )
    for other, device in others:
        send(1, lab_all.at[chip], lab_all.at[chip], device)
    arrived(1, lab_all.at[pl.ds(0, chips - 1)])

    place = lab_all[...].reshape(sources, blocks) - me * owned
    match = (place >= 0) & (place < owned)
    key = (iota((sources, blocks), 1) * owned + place).astype(F32)
    first = jnp.min(jnp.where(match, key, ABSENT), axis=1, keepdims=True)
    last = jnp.max(jnp.where(match, key, -1.0), axis=1, keepdims=True)
    size_f = float(owned)
    place_0 = jnp.where(first < ABSENT, first - jnp.floor(first / size_f) * size_f, -1.0)
    place_1 = jnp.where(last > first, last - jnp.floor(last / size_f) * size_f, -1.0)
    wanted = jnp.sum(
        jnp.where(
            iota((1, sources), 1) == slot_source,
            jnp.where(slot_rank == 0, to_row(place_0), to_row(place_1)),
            0.0,
        ),
        axis=1,
        keepdims=True,
    )
    picks = jnp.where(iota((1, owned), 1).astype(F32) == wanted, 1.0, 0.0).astype(BF16)
    inputs[2].wait()
    row_s[...] = dot(picks, field_v[...]).astype(BF16).reshape(2, chips, 2, width)
    for other, device in others:
        send(2, row_s.at[:, other], row_r.at[:, chip], device)
    row_r[:, chip] = row_s[:, chip]
    lane = iota((1, slots), 1)
    given = jnp.sum(
        jnp.where(
            iota((sources, 1), 0) == (lane >> 1),
            jnp.where((lane & 1) == 0, place_0, place_1),
            0.0,
        ),
        axis=0,
        keepdims=True,
    )
    deposits = jnp.where(iota((owned, 1), 0).astype(F32) == given, 1.0, 0.0).astype(BF16)
    arrived(2, row_r.at[:, pl.ds(0, chips - 1)])
    copy = send(3, row_r.at[1 - core], row_x, sibling)
    gas = dot(from_slots[:, :sources], row_r[core].reshape(sources, width))
    copy.wait()

    gas = gas + dot(from_slots[:, sources:], row_x[...].reshape(sources, width))
    gas = dot(gas.astype(BF16), spread)
    for copy in inputs[3:]:
        copy.wait()
    pair = 2 * cells
    sampled = []
    for g in range(blocks // 8):
        left = []
        for c in range(4):
            piece = gas[8 * g : 8 * g + 8, c * pair : (c + 1) * pair]
            left.append(
                jnp.where(diagonal, jnp.concatenate([piece] * 4, axis=1), 0.0)
            )
        left = jnp.concatenate(left, axis=0).astype(BF16)
        sampled.append(
            dot(left, tiles[8 * g : 8 * g + 8].reshape(8 * cells, parcels))
        )
    scale = 2.0 / cells
    u = [
        jnp.concatenate([s[8 * c : 8 * c + 8] for s in sampled], axis=0) * scale
        for c in range(4)
    ]

    v = [speed[c] for c in range(3)]
    d = size[...]
    t = heat[...]
    slip = [u[c] - v[c] for c in range(3)]
    slip_speed = jnp.sqrt(
        1.0 + (slip[0] * slip[0] + slip[1] * slip[1] + slip[2] * slip[2])
    )
    reynolds = REYNOLDS_SCALE * d * slip_speed
    squared = d * d
    drag = DRAG_SCALE * (1.0 + 0.15 * jnp.exp(0.687 * jnp.log(reynolds))) / squared
    warm = HEAT_SCALE * (2.0 + 0.6 * PRANDTL_ROOT * jnp.sqrt(reynolds)) / squared
    mass = LOADING * d * squared
    live_column = slot_column >= 0.0
    terms = []
    for c in range(3):
        new = (v[c] + drag * u[c]) / (1.0 + drag)
        terms.append((-mass * (new - v[c])).astype(BF16))
        moved[c] = jnp.where(live_column, new, v[c])
    new = (t + warm * u[3]) / (1.0 + warm)
    terms.append((-mass * (new - t)).astype(BF16))
    warmed[...] = jnp.where(live_column, new, t)
    outputs = [
        pltpu.make_async_copy(src, dst, out_sem.at[i])
        for i, (src, dst) in enumerate(((moved, moved_hbm), (warmed, warmed_hbm)))
    ]
    for copy in outputs:
        copy.start()

    lane, line = iota((32, pair), 1), iota((32, pair), 0)
    line = line & 7
    low = iota((8, pair), 1) < cells
    rows = []
    termf = [x.astype(F32) for x in terms]
    for g in range(blocks // 8):
        left = jnp.concatenate([x[8 * g : 8 * g + 8] for x in termf], axis=0)
        full = lax.dot_general(
            left.astype(BF16),
            tiles[8 * g : 8 * g + 8].reshape(8 * cells, parcels),
            (((1,), (1,)), ((), ())),
            preferred_element_type=F32,
        )
        own = jnp.zeros((32, pair), F32)
        for j in range(4):
            keep = line == 2 * j + lane // cells
            own = own + jnp.where(keep, full[:, j * pair : (j + 1) * pair], 0.0)
        own = own + pltpu.roll(own, cells, axis=1)
        rows.append(
            jnp.concatenate(
                [
                    jnp.where(low, own[0:8], own[8:16]),
                    jnp.where(low, own[16:24], own[24:32]),
                ],
                axis=1,
            )
        )
    high, rest = halves(jnp.concatenate(rows, axis=0) * scale)

    leave = to_slots[sources:]
    sums_x[...] = (dot(leave, high) + dot(leave, rest)).reshape(chips, 2, width)
    copy = send(4, sums_x, sums_s.at[:, core], sibling)
    stay = to_slots[:sources]
    sums_s[:, core] = (dot(stay, high) + dot(stay, rest)).reshape(chips, 2, width)
    copy.wait()
    for other, device in others:
        send(5, sums_s.at[other], sums_r.at[chip], device)
    sums_r[chip] = sums_s[chip]
    arrived(5, sums_r.at[pl.ds(0, chips - 1)])

    high, rest = halves(sums_r[...].reshape(slots, width))
    total = dot(deposits, high) + dot(deposits, rest)
    part_s[...] = total.reshape(nrep, owned // nrep, width)
    for other, device in reps:
        send(6, part_s.at[other], part_r.at[r], device)
    part_r[r] = part_s[r]
    arrived(6, part_r.at[pl.ds(0, nrep - 1)])
    total = part_r[0]
    for k in range(1, nrep):
        total = total + part_r[k]
    source_ref[...] = total
    for copy in outputs:
        copy.wait()


def per_device(
    ny,
    nz,
    nrep,
    particle_speeds,
    particle_diameters,
    particle_kelvins,
    unscaled_kernel_coefficients,
    bundle_patch_ordinal,
    bundle_patch_custodian,
    busy_bundles_per_accelerator,
    ambient_flow_quantities,
):
    blocks, cells, parcels = unscaled_kernel_coefficients.shape
    owned, width = ambient_flow_quantities.shape
    chips = ny * nz
    hbm = pl.BlockSpec(memory_space=pltpu.HBM)
    vmem = pl.BlockSpec(memory_space=pltpu.VMEM)
    smem = pl.BlockSpec(memory_space=pltpu.SMEM)
    moved, warmed, source = pl.pallas_call(
        functools.partial(step_kernel, ny, nz, nrep),
        out_shape=(
            jax.ShapeDtypeStruct((3, blocks, parcels), F32),
            jax.ShapeDtypeStruct((blocks, parcels), F32),
            jax.ShapeDtypeStruct((owned // nrep, width), F32),
        ),
        in_specs=[hbm, hbm, smem] + [hbm] * 5,
        out_specs=(hbm, hbm, vmem),
        scratch_shapes=[
            pltpu.VMEM((1, blocks), I32),
            pltpu.VMEM((1, blocks), I32),
            pltpu.VMEM((owned, width), BF16),
            pltpu.VMEM((blocks, cells, parcels), BF16),
            pltpu.VMEM((3, blocks, parcels), F32),
            pltpu.VMEM((blocks, parcels), F32),
            pltpu.VMEM((blocks, parcels), F32),
            pltpu.VMEM((3, blocks, parcels), F32),
            pltpu.VMEM((blocks, parcels), F32),
            pltpu.VMEM((1, blocks), I32),
            pltpu.VMEM((1, blocks), I32),
            pltpu.VMEM((chips, 2, blocks), I32),
            pltpu.VMEM((2, chips, 2, width), BF16),
            pltpu.VMEM((2, chips, 2, width), BF16),
            pltpu.VMEM((chips, 2, width), BF16),
            pltpu.VMEM((chips, 2, width), F32),
            pltpu.VMEM((chips, 2, 2, width), F32),
            pltpu.VMEM((chips, 2, 2, width), F32),
            pltpu.VMEM((nrep, owned // nrep, width), F32),
            pltpu.VMEM((nrep, owned // nrep, width), F32),
            pltpu.SemaphoreType.DMA((7,)),
            pltpu.SemaphoreType.DMA((2,)),
            pltpu.SemaphoreType.DMA((7,)),
            pltpu.SemaphoreType.DMA((7,)),
        ],
        compiler_params=pltpu.CompilerParams(
            collective_id=0, has_side_effects=True, vmem_limit_bytes=63 * 2**20
        ),
        name="parcel_step",
    )(
        bundle_patch_custodian.reshape(1, blocks),
        bundle_patch_ordinal.reshape(1, blocks),
        busy_bundles_per_accelerator,
        ambient_flow_quantities,
        unscaled_kernel_coefficients,
        jnp.transpose(particle_speeds, (1, 0, 2)),
        particle_diameters,
        particle_kelvins,
    )
    return jnp.transpose(moved, (1, 0, 2)), warmed, source


def solution(mesh, ny=4, nz=16):
    both = ("cells", "rep")
    return jax.shard_map(
        functools.partial(per_device, ny, nz, mesh.shape["rep"]),
        mesh=mesh,
        in_specs=(
            P(both, None, None),
            P(both, None),
            P(both, None),
            P(both, None, None),
            P(both),
            P(both),
            P(both),
            P("cells", None),
        ),
        out_specs=(P(both, None, None), P(both, None), P(both, None)),
        check_vma=False,
    )
```

time: 78.9 us -> 66.9 us (0.85)
  Pallas kernels: 67.9 us -> 60.3 us
  local copies, waits for them, and re-layouts: 8.34 us -> 4.56 us
    pallas_call x1, Pallas kernels: 67.9 us -> 60.3 us  [per_device(): pl.pallas_call(functools.partial(step_kernel, ny, nz, nrep), out_shape=(j...]
    unnamed x17 -> x3, local copies, waits for them, and re-layouts: 8.34 us -> 4.56 us
where the time goes in v2:
time: 66.9 us; the launch traced here: 66.2 us
  Pallas kernels  60.3 us (90%)
  local copies, waits for them, and re-layouts  4.56 us (7%)
  between operations  1.29 us (2%)
    pallas_call x1, Pallas kernels, per_device(): pl.pallas_call(functools.partial(step_kernel, ny, nz, nrep), out_shape=(j...  60.3 us
    unnamed x3, local copies, waits for them, and re-layouts  4.56 us

profile of v2, /device:TPU:1, one launch (start us, length us, event | category | flops | bytes accessed | tf_op | source)
XLA Modules:
  0.0 66.2 jit_solution(5109256854975449411)
XLA Ops:
  1.3 60.3 %parcel_step.1 = (f32[3,128,128]{2,1,0:T(8,128)}, f32[128,128]{1,0:T(8,128)}, f32[64,256]{1,0:T(8,128)}) custom-call(s32[1,128]{1,0:T(1,128)} %bitcast.6, s32[1,128]{1,0:T(1,128)} %bitcast.7, s32[1]{0:T(128)S(6)} %copy.14.busy_ref, bf16[256,256]{1,0:T(8,128)(2,1)} %field_hbm.1, bf16[128,64,128]{2,1,0:T(8,128)(2,1)} %tiles_hbm.1, f32[3,128,128]{2,1,0:T(8,128)} %bitcast.5, ...), custom_call_target="tpu_custom_call" | custom-call | tf_op jit(solution)/shard_map/parcel_step/pallas_call | solution.py:363
  61.6 1.6 %copy.15 = f32[128,3,128]{2,0,1:T(8,128)} copy(f32[128,3,128]{2,0,1:T(8,128)} %bitcast.4) | data formatting | bytes 393216
  63.2 1.5 %copy.16 = f32[128,128]{1,0:T(8,128)} copy(f32[128,128]{1,0:T(8,128)} %get-tuple-element.13) | data formatting | bytes 131072
  64.7 1.5 %copy.17 = f32[64,256]{1,0:T(8,128)} copy(f32[64,256]{1,0:T(8,128)} %get-tuple-element.14) | data formatting | bytes 131072

commit v3 on v2

--- a/solution.py
+++ b/solution.py
@@ -1,4 +1,5 @@
 import functools
+import math
 
 import jax
 import jax.numpy as jnp
@@ -8,7 +9,7 @@
 from jax.sharding import PartitionSpec as P
 
 MESH = pl.DeviceIdType.MESH
-F32, BF16, I32 = jnp.float32, jnp.bfloat16, jnp.int32
+F32, BF16, I32, I16 = jnp.float32, jnp.bfloat16, jnp.int32, jnp.int16
 
 REYNOLDS_SCALE = 20.0
 DRAG_SCALE = 1.0
@@ -16,6 +17,9 @@
 PRANDTL_ROOT = 0.9
 LOADING = 0.2
 ABSENT = 1.0e9
+LARGEST = 512.0
+OCTAVES = 32
+CODES = 1023.5
 
 
 def iota(shape, axis):
@@ -37,6 +41,20 @@
 def halves(x):
     high = x.astype(BF16)
     return high, (x - high.astype(F32)).astype(BF16)
+
+
+def encode(x):
+    least = LARGEST / 2.0**OCTAVES
+    code = jnp.log(1.0 + jnp.abs(x) * (1.0 / least)) * (CODES / math.log(2.0))
+    code = jnp.where(x < 0.0, -code, code)
+    return jnp.round(code).astype(I32).astype(I16)
+
+
+def decode(code):
+    least = LARGEST / 2.0**OCTAVES
+    code = code.astype(I32).astype(F32)
+    size = jnp.exp(jnp.abs(code) * (math.log(2.0) / CODES)) * least - least
+    return jnp.where(code < 0.0, -size, size)
 
 
 def dot(a, b):
@@ -67,12 +85,11 @@
     heat,
     moved,
     warmed,
-    lab_mine,
-    lab_other,
+    field_x,
     lab_all,
+    lab_x,
     row_s,
     row_r,
-    row_x,
     sums_x,
     sums_s,
     sums_r,
@@ -160,15 +177,14 @@
     spread = jnp.where(iota((width, 8 * cells), 0) == target, 1.0, 0.0).astype(BF16)
     diagonal = (iota((1, 8 * cells), 1) // cells) == iota((8, 1), 0)
     slot_line = iota((slots, 1), 0)
-    slot_rank = slot_line & 1
-    slot_source = ((slot_line & (sources - 1)) >> 1) * 2 + slot_line // sources
+    pair_line = iota((sources, 1), 0)
 
     inputs[0].wait()
     inputs[1].wait()
     owner = owner_v[...]
     live = iota((1, blocks), 1) < busy_ref[0]
     label = jnp.where(live, owner * owned + place_v[...], -1)
-    lab_mine[...] = label
+    lab_all[chip] = label
 
     ownerf = owner.astype(F32)
     earlier = (
@@ -187,55 +203,62 @@
 
     pl.semaphore_wait(barrier, chips - 1 + nrep - 1 + 1)
 
-    send(0, lab_mine, lab_other, sibling).wait()
-    got = lab_other[...]
-    lab_all[chip] = jnp.concatenate(
-        [jnp.where(core == 0, label, got), jnp.where(core == 0, got, label)], axis=0
-    )
     for other, device in others:
-        send(1, lab_all.at[chip], lab_all.at[chip], device)
-    arrived(1, lab_all.at[pl.ds(0, chips - 1)])
-
-    place = lab_all[...].reshape(sources, blocks) - me * owned
-    match = (place >= 0) & (place < owned)
-    key = (iota((sources, blocks), 1) * owned + place).astype(F32)
-    first = jnp.min(jnp.where(match, key, ABSENT), axis=1, keepdims=True)
-    last = jnp.max(jnp.where(match, key, -1.0), axis=1, keepdims=True)
-    size_f = float(owned)
-    place_0 = jnp.where(first < ABSENT, first - jnp.floor(first / size_f) * size_f, -1.0)
-    place_1 = jnp.where(last > first, last - jnp.floor(last / size_f) * size_f, -1.0)
-    wanted = jnp.sum(
-        jnp.where(
-            iota((1, sources), 1) == slot_source,
-            jnp.where(slot_rank == 0, to_row(place_0), to_row(place_1)),
-            0.0,
-        ),
-        axis=1,
-        keepdims=True,
-    )
-    picks = jnp.where(iota((1, owned), 1).astype(F32) == wanted, 1.0, 0.0).astype(BF16)
+        send(0, lab_all.at[chip], lab_all.at[chip], device)
     inputs[2].wait()
-    row_s[...] = dot(picks, field_v[...]).astype(BF16).reshape(2, chips, 2, width)
+    fields = send(1, field_v, field_x, sibling)
+
+    def find(table, owner_id):
+        place = table[...].reshape(chips, blocks) - owner_id * owned
+        match = (place >= 0) & (place < owned)
+        key = (iota((chips, blocks), 1) * owned + place).astype(F32)
+        first = jnp.min(jnp.where(match, key, ABSENT), axis=1, keepdims=True)
+        last = jnp.max(jnp.where(match, key, -1.0), axis=1, keepdims=True)
+        size_f = float(owned)
+        place_0 = first - jnp.floor(first / size_f) * size_f
+        place_1 = last - jnp.floor(last / size_f) * size_f
+        return (
+            jnp.where(first < ABSENT, place_0, -1.0),
+            jnp.where(last > first, place_1, -1.0),
+        )
+
+    arrived(0, lab_all.at[pl.ds(0, chips - 1)])
+    labels = send(2, lab_all, lab_x, sibling)
+
+    found = [find(lab_all, me), find(lab_all, chip * 2 + (1 - core))]
+    fields.wait()
+    for i, (places, field) in enumerate(zip(found, (field_v, field_x))):
+        wanted = jnp.sum(
+            jnp.where(
+                iota((1, chips), 1) == (pair_line >> 1),
+                jnp.where((pair_line & 1) == 0, to_row(places[0]), to_row(places[1])),
+                0.0,
+            ),
+            axis=1,
+            keepdims=True,
+        )
+        picks = jnp.where(iota((1, owned), 1).astype(F32) == wanted, 1.0, 0.0)
+        rows = dot(picks.astype(BF16), field[...]).astype(BF16)
+        row_s[i] = rows.reshape(chips, 2, width)
     for other, device in others:
-        send(2, row_s.at[:, other], row_r.at[:, chip], device)
+        send(3, row_s.at[:, other], row_r.at[:, chip], device)
     row_r[:, chip] = row_s[:, chip]
+
+    labels.wait()
     lane = iota((1, slots), 1)
+    here, there = found[0], find(lab_x, me)
+    given = jnp.where(
+        (lane & 2) == 0,
+        jnp.where((lane & 1) == 0, here[0], here[1]),
+        jnp.where((lane & 1) == 0, there[0], there[1]),
+    )
     given = jnp.sum(
-        jnp.where(
-            iota((sources, 1), 0) == (lane >> 1),
-            jnp.where((lane & 1) == 0, place_0, place_1),
-            0.0,
-        ),
-        axis=0,
-        keepdims=True,
+        jnp.where(iota((chips, 1), 0) == (lane >> 2), given, 0.0), axis=0, keepdims=True
     )
     deposits = jnp.where(iota((owned, 1), 0).astype(F32) == given, 1.0, 0.0).astype(BF16)
-    arrived(2, row_r.at[:, pl.ds(0, chips - 1)])
-    copy = send(3, row_r.at[1 - core], row_x, sibling)
-    gas = dot(from_slots[:, :sources], row_r[core].reshape(sources, width))
-    copy.wait()
-
-    gas = gas + dot(from_slots[:, sources:], row_x[...].reshape(sources, width))
+    arrived(3, row_r.at[:, pl.ds(0, chips - 1)])
+
+    gas = dot(from_slots, row_r[...].reshape(slots, width))
     gas = dot(gas.astype(BF16), spread)
     for copy in inputs[3:]:
         copy.wait()
@@ -316,17 +339,17 @@
     high, rest = halves(jnp.concatenate(rows, axis=0) * scale)
 
     leave = to_slots[sources:]
-    sums_x[...] = (dot(leave, high) + dot(leave, rest)).reshape(chips, 2, width)
-    copy = send(4, sums_x, sums_s.at[:, core], sibling)
+    sums_x[...] = encode(dot(leave, high) + dot(leave, rest)).reshape(chips, 2, width)
+    copy = send(4, sums_x, sums_s.at[:, 1], sibling)
     stay = to_slots[:sources]
-    sums_s[:, core] = (dot(stay, high) + dot(stay, rest)).reshape(chips, 2, width)
+    sums_s[:, 0] = encode(dot(stay, high) + dot(stay, rest)).reshape(chips, 2, width)
     copy.wait()
     for other, device in others:
         send(5, sums_s.at[other], sums_r.at[chip], device)
     sums_r[chip] = sums_s[chip]
     arrived(5, sums_r.at[pl.ds(0, chips - 1)])
 
-    high, rest = halves(sums_r[...].reshape(slots, width))
+    high, rest = halves(decode(sums_r[...].reshape(slots, width)))
     total = dot(deposits, high) + dot(deposits, rest)
     part_s[...] = total.reshape(nrep, owned // nrep, width)
     for other, device in reps:
@@ -338,6 +361,17 @@
         total = total + part_r[k]
     source_ref[...] = total
     for copy in outputs:
+        copy.wait()
+
+
+def hand_over(count, *refs):
+    copies = [
+        pltpu.make_async_copy(refs[i], refs[count + i], refs[2 * count].at[i])
+        for i in range(count)
+    ]
+    for copy in copies:
+        copy.start()
+    for copy in copies:
         copy.wait()
 
 
@@ -360,7 +394,7 @@
     hbm = pl.BlockSpec(memory_space=pltpu.HBM)
     vmem = pl.BlockSpec(memory_space=pltpu.VMEM)
     smem = pl.BlockSpec(memory_space=pltpu.SMEM)
-    moved, warmed, source = pl.pallas_call(
+    results = pl.pallas_call(
         functools.partial(step_kernel, ny, nz, nrep),
         out_shape=(
             jax.ShapeDtypeStruct((3, blocks, parcels), F32),
@@ -379,15 +413,14 @@
             pltpu.VMEM((blocks, parcels), F32),
             pltpu.VMEM((3, blocks, parcels), F32),
             pltpu.VMEM((blocks, parcels), F32),
-            pltpu.VMEM((1, blocks), I32),
-            pltpu.VMEM((1, blocks), I32),
-            pltpu.VMEM((chips, 2, blocks), I32),
+            pltpu.VMEM((owned, width), BF16),
+            pltpu.VMEM((chips, 1, blocks), I32),
+            pltpu.VMEM((chips, 1, blocks), I32),
             pltpu.VMEM((2, chips, 2, width), BF16),
             pltpu.VMEM((2, chips, 2, width), BF16),
-            pltpu.VMEM((chips, 2, width), BF16),
-            pltpu.VMEM((chips, 2, width), F32),
-            pltpu.VMEM((chips, 2, 2, width), F32),
-            pltpu.VMEM((chips, 2, 2, width), F32),
+            pltpu.VMEM((chips, 2, width), I16),
+            pltpu.VMEM((chips, 2, 2, width), I16),
+            pltpu.VMEM((chips, 2, 2, width), I16),
             pltpu.VMEM((nrep, owned // nrep, width), F32),
             pltpu.VMEM((nrep, owned // nrep, width), F32),
             pltpu.SemaphoreType.DMA((7,)),
@@ -409,6 +442,15 @@
         particle_diameters,
         particle_kelvins,
     )
+    moved, warmed, source = pl.pallas_call(
+        functools.partial(hand_over, 3),
+        out_shape=tuple(jax.ShapeDtypeStruct(x.shape, x.dtype) for x in results),
+        in_specs=[hbm] * 3,
+        out_specs=(hbm, hbm, hbm),
+        scratch_shapes=[pltpu.SemaphoreType.DMA((3,))],
+        compiler_params=pltpu.CompilerParams(vmem_limit_bytes=63 * 2**20),
+        name="hand_over",
+    )(*results)
     return jnp.transpose(moved, (1, 0, 2)), warmed, source
 
 

time: 66.9 us -> 66 us (0.987)
  local copies, waits for them, and re-layouts: 4.56 us -> 0 us
  Pallas kernels: 60.3 us -> 64.5 us
    pallas_call x0 -> x1, Pallas kernels: none -> 11.1 us  [per_device(): pl.pallas_call(functools.partial(hand_over, 3), out_shape=tuple((jax.Shap...]
    pallas_call x1, Pallas kernels: 60.3 us -> 53.4 us  [per_device(): pl.pallas_call(functools.partial(step_kernel, ny, nz, nrep), out_shape=(j...]
    unnamed x3 -> x0, local copies, waits for them, and re-layouts: 4.56 us -> none
where the time goes in v3:
time: 66 us; the launch traced here: 65.8 us
  Pallas kernels  64.5 us (98%)
  between operations  1.29 us (2%)
    pallas_call x1, Pallas kernels, per_device(): pl.pallas_call(functools.partial(step_kernel, ny, nz, nrep), out_shape=(j...  53.4 us
    pallas_call x1, Pallas kernels, per_device(): pl.pallas_call(functools.partial(hand_over, 3), out_shape=tuple((jax.Shap...  11.1 us

profile of v3, /device:TPU:1, one launch (start us, length us, event | category | flops | bytes accessed | tf_op | source)
XLA Modules:
  0.0 65.8 jit_solution(1343080897852153705)
XLA Ops:
  1.3 53.4 %parcel_step.1 = (f32[3,128,128]{2,1,0:T(8,128)}, f32[128,128]{1,0:T(8,128)}, f32[64,256]{1,0:T(8,128)}) custom-call(s32[1,128]{1,0:T(1,128)} %bitcast.5, s32[1,128]{1,0:T(1,128)} %bitcast.6, s32[1]{0:T(128)S(6)} %copy.11.busy_ref, bf16[256,256]{1,0:T(8,128)(2,1)} %field_hbm.1, bf16[128,64,128]{2,1,0:T(8,128)(2,1)} %tiles_hbm.1, f32[3,128,128]{2,1,0:T(8,128)} %bitcast.4, ...), custom_call_target="tpu_custom_call" | custom-call | tf_op jit(solution)/shard_map/parcel_step/pallas_call | solution.py:397
  54.7 11.1 %hand_over.1 = (f32[3,128,128]{2,1,0:T(8,128)}, f32[128,128]{1,0:T(8,128)}, f32[64,256]{1,0:T(8,128)}) custom-call(f32[3,128,128]{2,1,0:T(8,128)} %get-tuple-element.9.refs_0_, f32[128,128]{1,0:T(8,128)} %get-tuple-element.10.refs_1_, f32[64,256]{1,0:T(8,128)} %get-tuple-element.11.refs_2_), custom_call_target="tpu_custom_call" | custom-call | tf_op jit(solution)/shard_map/hand_over/pallas_call | solution.py:445

commit v4 on v3

--- a/solution.py
+++ b/solution.py
@@ -46,8 +46,7 @@
 def encode(x):
     least = LARGEST / 2.0**OCTAVES
     code = jnp.log(1.0 + jnp.abs(x) * (1.0 / least)) * (CODES / math.log(2.0))
-    code = jnp.where(x < 0.0, -code, code)
-    return jnp.round(code).astype(I32).astype(I16)
+    return jnp.round(jnp.where(x < 0.0, -code, code))
 
 
 def decode(code):
@@ -143,12 +142,14 @@
             )
         )
     ]
-    for copy in inputs:
+    for copy in inputs[:3]:
         copy.start()
 
     barrier = pltpu.get_barrier_semaphore()
     for device in [device for _, device in others + reps] + [sibling]:
         pl.semaphore_signal(barrier, inc=1, device_id=device, device_id_type=MESH)
+    for copy in inputs[3:]:
+        copy.start()
 
     def send(phase, src, dst, device):
         copy = pltpu.make_async_remote_copy(
@@ -177,7 +178,6 @@
     spread = jnp.where(iota((width, 8 * cells), 0) == target, 1.0, 0.0).astype(BF16)
     diagonal = (iota((1, 8 * cells), 1) // cells) == iota((8, 1), 0)
     slot_line = iota((slots, 1), 0)
-    pair_line = iota((sources, 1), 0)
 
     inputs[0].wait()
     inputs[1].wait()
@@ -208,55 +208,49 @@
     inputs[2].wait()
     fields = send(1, field_v, field_x, sibling)
 
-    def find(table, owner_id):
-        place = table[...].reshape(chips, blocks) - owner_id * owned
+    second = (iota((sources, blocks), 0) & 1) == 1
+    key_lane = iota((sources, blocks), 1) * owned
+
+    def spread_out(table):
+        return jnp.broadcast_to(table[...], (chips, 2, blocks)).reshape(sources, blocks)
+
+    def find(labels, owner_id):
+        place = labels - owner_id * owned
         match = (place >= 0) & (place < owned)
-        key = (iota((chips, blocks), 1) * owned + place).astype(F32)
-        first = jnp.min(jnp.where(match, key, ABSENT), axis=1, keepdims=True)
-        last = jnp.max(jnp.where(match, key, -1.0), axis=1, keepdims=True)
-        size_f = float(owned)
-        place_0 = first - jnp.floor(first / size_f) * size_f
-        place_1 = last - jnp.floor(last / size_f) * size_f
-        return (
-            jnp.where(first < ABSENT, place_0, -1.0),
-            jnp.where(last > first, place_1, -1.0),
-        )
+        key = (key_lane + place).astype(F32)
+        key = jnp.where(match, jnp.where(second, -key, key), ABSENT)
+        key = jnp.abs(jnp.min(key, axis=1, keepdims=True))
+        return key - jnp.floor(key * (1.0 / owned)) * owned
 
     arrived(0, lab_all.at[pl.ds(0, chips - 1)])
     labels = send(2, lab_all, lab_x, sibling)
 
-    found = [find(lab_all, me), find(lab_all, chip * 2 + (1 - core))]
+    table = spread_out(lab_all)
+    field_lane = iota((1, owned), 1).astype(F32)
+
+    def serve(i, place, field):
+        picks = jnp.where(field_lane == place, 1.0, 0.0).astype(BF16)
+        row_s[i] = dot(picks, field[...]).astype(BF16).reshape(chips, 2, width)
+        for other, device in others:
+            send(3 + i, row_s.at[i, other], row_r.at[i, chip], device)
+        row_r[i, chip] = row_s[i, chip]
+
+    here = find(table, me)
+    serve(0, here, field_v)
+    place = find(table, chip * 2 + (1 - core))
     fields.wait()
-    for i, (places, field) in enumerate(zip(found, (field_v, field_x))):
-        wanted = jnp.sum(
+    serve(1, place, field_x)
+
+    labels.wait()
+    deposits = []
+    for place in (here, find(spread_out(lab_x), me)):
+        deposits.append(
             jnp.where(
-                iota((1, chips), 1) == (pair_line >> 1),
-                jnp.where((pair_line & 1) == 0, to_row(places[0]), to_row(places[1])),
-                0.0,
-            ),
-            axis=1,
-            keepdims=True,
-        )
-        picks = jnp.where(iota((1, owned), 1).astype(F32) == wanted, 1.0, 0.0)
-        rows = dot(picks.astype(BF16), field[...]).astype(BF16)
-        row_s[i] = rows.reshape(chips, 2, width)
-    for other, device in others:
-        send(3, row_s.at[:, other], row_r.at[:, chip], device)
-    row_r[:, chip] = row_s[:, chip]
-
-    labels.wait()
-    lane = iota((1, slots), 1)
-    here, there = found[0], find(lab_x, me)
-    given = jnp.where(
-        (lane & 2) == 0,
-        jnp.where((lane & 1) == 0, here[0], here[1]),
-        jnp.where((lane & 1) == 0, there[0], there[1]),
-    )
-    given = jnp.sum(
-        jnp.where(iota((chips, 1), 0) == (lane >> 2), given, 0.0), axis=0, keepdims=True
-    )
-    deposits = jnp.where(iota((owned, 1), 0).astype(F32) == given, 1.0, 0.0).astype(BF16)
-    arrived(3, row_r.at[:, pl.ds(0, chips - 1)])
+                iota((owned, 1), 0).astype(F32) == to_row(place), 1.0, 0.0
+            ).astype(BF16)
+        )
+    for i in range(2):
+        arrived(3 + i, row_r.at[i, pl.ds(0, chips - 1)])
 
     gas = dot(from_slots, row_r[...].reshape(slots, width))
     gas = dot(gas.astype(BF16), spread)
@@ -336,26 +330,34 @@
                 axis=1,
             )
         )
-    high, rest = halves(jnp.concatenate(rows, axis=0) * scale)
-
-    leave = to_slots[sources:]
-    sums_x[...] = encode(dot(leave, high) + dot(leave, rest)).reshape(chips, 2, width)
-    copy = send(4, sums_x, sums_s.at[:, 1], sibling)
-    stay = to_slots[:sources]
-    sums_s[:, 0] = encode(dot(stay, high) + dot(stay, rest)).reshape(chips, 2, width)
-    copy.wait()
-    for other, device in others:
-        send(5, sums_s.at[other], sums_r.at[chip], device)
-    sums_r[chip] = sums_s[chip]
-    arrived(5, sums_r.at[pl.ds(0, chips - 1)])
-
-    high, rest = halves(decode(sums_r[...].reshape(slots, width)))
-    total = dot(deposits, high) + dot(deposits, rest)
+    code = encode(jnp.concatenate(rows, axis=0) * scale)
+    high = jnp.floor(code * (1.0 / 256.0)) * 256.0
+    code = [high.astype(BF16), (code - high).astype(BF16)]
+
+    def in_slots(lines):
+        code_there = dot(lines, code[0]) + dot(lines, code[1])
+        return code_there.astype(I32).astype(I16).reshape(chips, 2, width)
+
+    sums_x[...] = in_slots(to_slots[sources:])
+    copy = send(5, sums_x, sums_s.at[1], sibling)
+    sums_s[0] = in_slots(to_slots[:sources])
+    for i in range(2):
+        if i == 1:
+            copy.wait()
+        for other, device in others:
+            send(6 + i, sums_s.at[i, other], sums_r.at[i, chip], device)
+        sums_r[i, chip] = sums_s[i, chip]
+
+    total = jnp.zeros((owned, width), F32)
+    for i in range(2):
+        arrived(6 + i, sums_r.at[i, pl.ds(0, chips - 1)])
+        high, rest = halves(decode(sums_r[i].reshape(sources, width)))
+        total = total + dot(deposits[i], high) + dot(deposits[i], rest)
     part_s[...] = total.reshape(nrep, owned // nrep, width)
     for other, device in reps:
-        send(6, part_s.at[other], part_r.at[r], device)
+        send(8, part_s.at[other], part_r.at[r], device)
     part_r[r] = part_s[r]
-    arrived(6, part_r.at[pl.ds(0, nrep - 1)])
+    arrived(8, part_r.at[pl.ds(0, nrep - 1)])
     total = part_r[0]
     for k in range(1, nrep):
         total = total + part_r[k]
@@ -365,13 +367,20 @@
 
 
 def hand_over(count, *refs):
-    copies = [
-        pltpu.make_async_copy(refs[i], refs[count + i], refs[2 * count].at[i])
-        for i in range(count)
+    sources, results, held = (refs[i * count : (i + 1) * count] for i in range(3))
+    sem_in, sem_out = refs[3 * count :]
+    arrive = [
+        pltpu.make_async_copy(sources[i], held[i], sem_in.at[i]) for i in range(count)
     ]
-    for copy in copies:
+    leave = [
+        pltpu.make_async_copy(held[i], results[i], sem_out.at[i]) for i in range(count)
+    ]
+    for copy in arrive:
         copy.start()
-    for copy in copies:
+    for i in range(count):
+        arrive[i].wait()
+        leave[i].start()
+    for copy in leave:
         copy.wait()
 
 
@@ -419,14 +428,14 @@
             pltpu.VMEM((2, chips, 2, width), BF16),
             pltpu.VMEM((2, chips, 2, width), BF16),
             pltpu.VMEM((chips, 2, width), I16),
-            pltpu.VMEM((chips, 2, 2, width), I16),
-            pltpu.VMEM((chips, 2, 2, width), I16),
+            pltpu.VMEM((2, chips, 2, width), I16),
+            pltpu.VMEM((2, chips, 2, width), I16),
             pltpu.VMEM((nrep, owned // nrep, width), F32),
             pltpu.VMEM((nrep, owned // nrep, width), F32),
             pltpu.SemaphoreType.DMA((7,)),
             pltpu.SemaphoreType.DMA((2,)),
-            pltpu.SemaphoreType.DMA((7,)),
-            pltpu.SemaphoreType.DMA((7,)),
+            pltpu.SemaphoreType.DMA((9,)),
+            pltpu.SemaphoreType.DMA((9,)),
         ],
         compiler_params=pltpu.CompilerParams(
             collective_id=0, has_side_effects=True, vmem_limit_bytes=63 * 2**20
@@ -447,7 +456,8 @@
         out_shape=tuple(jax.ShapeDtypeStruct(x.shape, x.dtype) for x in results),
         in_specs=[hbm] * 3,
         out_specs=(hbm, hbm, hbm),
-        scratch_shapes=[pltpu.SemaphoreType.DMA((3,))],
+        scratch_shapes=[pltpu.VMEM(x.shape, x.dtype) for x in results]
+        + [pltpu.SemaphoreType.DMA((3,))] * 2,
         compiler_params=pltpu.CompilerParams(vmem_limit_bytes=63 * 2**20),
         name="hand_over",
     )(*results)

time: 66 us -> 57.4 us (0.87)
  the two profiles are of different devices: /device:TPU:1 before, /device:TPU:8 now
where the time goes in v4:
time: 57.4 us; the launch traced here: 57.2 us
  Pallas kernels  56 us (98%)
  between operations  1.29 us (2%)
    pallas_call x1, Pallas kernels, per_device(): pl.pallas_call(functools.partial(step_kernel, ny, nz, nrep), out_shape=(j...  54.3 us
    pallas_call x1, Pallas kernels, per_device(): pl.pallas_call(functools.partial(hand_over, 3), out_shape=tuple((jax.Shap...  1.69 us

profile of v4, /device:TPU:8, one launch (start us, length us, event | category | flops | bytes accessed | tf_op | source)
XLA Modules:
  0.0 57.2 jit_solution(2117496430726982542)
XLA Ops:
  1.3 54.3 %parcel_step.1 = (f32[3,128,128]{2,1,0:T(8,128)}, f32[128,128]{1,0:T(8,128)}, f32[64,256]{1,0:T(8,128)}) custom-call(s32[1,128]{1,0:T(1,128)} %bitcast.5, s32[1,128]{1,0:T(1,128)} %bitcast.6, s32[1]{0:T(128)S(6)} %copy.11.busy_ref, bf16[256,256]{1,0:T(8,128)(2,1)} %field_hbm.1, bf16[128,64,128]{2,1,0:T(8,128)(2,1)} %tiles_hbm.1, f32[3,128,128]{2,1,0:T(8,128)} %bitcast.4, ...), custom_call_target="tpu_custom_call" | custom-call | tf_op jit(solution)/shard_map/parcel_step/pallas_call | solution.py:406
  55.5 1.7 %hand_over.1 = (f32[3,128,128]{2,1,0:T(8,128)}, f32[128,128]{1,0:T(8,128)}, f32[64,256]{1,0:T(8,128)}) custom-call(f32[3,128,128]{2,1,0:T(8,128)} %get-tuple-element.9.refs_0_, f32[128,128]{1,0:T(8,128)} %get-tuple-element.10.refs_1_, f32[64,256]{1,0:T(8,128)} %get-tuple-element.11.refs_2_), custom_call_target="tpu_custom_call" | custom-call | tf_op jit(solution)/shard_map/hand_over/pallas_call | solution.py:454

commit v5 on v4

--- a/solution.py
+++ b/solution.py
@@ -228,18 +228,15 @@
     table = spread_out(lab_all)
     field_lane = iota((1, owned), 1).astype(F32)
 
-    def serve(i, place, field):
-        picks = jnp.where(field_lane == place, 1.0, 0.0).astype(BF16)
-        row_s[i] = dot(picks, field[...]).astype(BF16).reshape(chips, 2, width)
-        for other, device in others:
-            send(3 + i, row_s.at[i, other], row_r.at[i, chip], device)
-        row_r[i, chip] = row_s[i, chip]
-
     here = find(table, me)
-    serve(0, here, field_v)
     place = find(table, chip * 2 + (1 - core))
     fields.wait()
-    serve(1, place, field_x)
+    for i, (wanted, field) in enumerate(((here, field_v), (place, field_x))):
+        picks = jnp.where(field_lane == wanted, 1.0, 0.0).astype(BF16)
+        row_s[i] = dot(picks, field[...]).astype(BF16).reshape(chips, 2, width)
+    for other, device in others:
+        send(3, row_s.at[:, other], row_r.at[:, chip], device)
+    row_r[:, chip] = row_s[:, chip]
 
     labels.wait()
     deposits = []
@@ -249,8 +246,7 @@
                 iota((owned, 1), 0).astype(F32) == to_row(place), 1.0, 0.0
             ).astype(BF16)
         )
-    for i in range(2):
-        arrived(3 + i, row_r.at[i, pl.ds(0, chips - 1)])
+    arrived(3, row_r.at[:, pl.ds(0, chips - 1)])
 
     gas = dot(from_slots, row_r[...].reshape(slots, width))
     gas = dot(gas.astype(BF16), spread)

time: 57.4 us -> 55.3 us (0.963)
  the two profiles are of different devices: /device:TPU:8 before, /device:TPU:1 now
where the time goes in v5:
time: 55.3 us; the launch traced here: 54.9 us
  Pallas kernels  53.6 us (97%)
  between operations  1.29 us (2%)
    pallas_call x1, Pallas kernels, per_device(): pl.pallas_call(functools.partial(step_kernel, ny, nz, nrep), out_shape=(j...  51.9 us
    pallas_call x1, Pallas kernels, per_device(): pl.pallas_call(functools.partial(hand_over, 3), out_shape=tuple((jax.Shap...  1.69 us

profile of v5, /device:TPU:1, one launch (start us, length us, event | category | flops | bytes accessed | tf_op | source)
XLA Modules:
  0.0 54.9 jit_solution(14806168696040962494)
XLA Ops:
  1.3 51.9 %parcel_step.1 = (f32[3,128,128]{2,1,0:T(8,128)}, f32[128,128]{1,0:T(8,128)}, f32[64,256]{1,0:T(8,128)}) custom-call(s32[1,128]{1,0:T(1,128)} %bitcast.5, s32[1,128]{1,0:T(1,128)} %bitcast.6, s32[1]{0:T(128)S(6)} %copy.11.busy_ref, bf16[256,256]{1,0:T(8,128)(2,1)} %field_hbm.1, bf16[128,64,128]{2,1,0:T(8,128)(2,1)} %tiles_hbm.1, f32[3,128,128]{2,1,0:T(8,128)} %bitcast.4, ...), custom_call_target="tpu_custom_call" | custom-call | tf_op jit(solution)/shard_map/parcel_step/pallas_call | solution.py:402
  53.2 1.7 %hand_over.1 = (f32[3,128,128]{2,1,0:T(8,128)}, f32[128,128]{1,0:T(8,128)}, f32[64,256]{1,0:T(8,128)}) custom-call(f32[3,128,128]{2,1,0:T(8,128)} %get-tuple-element.9.refs_0_, f32[128,128]{1,0:T(8,128)} %get-tuple-element.10.refs_1_, f32[64,256]{1,0:T(8,128)} %get-tuple-element.11.refs_2_), custom_call_target="tpu_custom_call" | custom-call | tf_op jit(solution)/shard_map/hand_over/pallas_call | solution.py:450

commit v6 on v5

--- a/solution.py
+++ b/solution.py
@@ -20,6 +20,7 @@
 LARGEST = 512.0
 OCTAVES = 32
 CODES = 1023.5
+PART_CODES = 819.0
 
 
 def iota(shape, axis):
@@ -43,16 +44,16 @@
     return high, (x - high.astype(F32)).astype(BF16)
 
 
-def encode(x):
+def encode(x, codes=CODES):
     least = LARGEST / 2.0**OCTAVES
-    code = jnp.log(1.0 + jnp.abs(x) * (1.0 / least)) * (CODES / math.log(2.0))
+    code = jnp.log(1.0 + jnp.abs(x) * (1.0 / least)) * (codes / math.log(2.0))
     return jnp.round(jnp.where(x < 0.0, -code, code))
 
 
-def decode(code):
+def decode(code, codes=CODES):
     least = LARGEST / 2.0**OCTAVES
     code = code.astype(I32).astype(F32)
-    size = jnp.exp(jnp.abs(code) * (math.log(2.0) / CODES)) * least - least
+    size = jnp.exp(jnp.abs(code) * (math.log(2.0) / codes)) * least - least
     return jnp.where(code < 0.0, -size, size)
 
 
@@ -92,6 +93,7 @@
     sums_x,
     sums_s,
     sums_r,
+    part_v,
     part_s,
     part_r,
     in_sem,
@@ -337,26 +339,31 @@
     sums_x[...] = in_slots(to_slots[sources:])
     copy = send(5, sums_x, sums_s.at[1], sibling)
     sums_s[0] = in_slots(to_slots[:sources])
+    far, near = others[: len(others) // 2], others[len(others) // 2 :]
+    for other, device in far:
+        send(6, sums_s.at[0, other], sums_r.at[0, chip], device)
+    copy.wait()
+    for other, device in far:
+        send(6, sums_s.at[1, other], sums_r.at[1, chip], device)
+    for other, device in near:
+        send(6, sums_s.at[:, other], sums_r.at[:, chip], device)
+    sums_r[:, chip] = sums_s[:, chip]
+
+    total = jnp.zeros((owned, width), F32)
+    arrived(6, sums_r.at[:, pl.ds(0, chips - 1)])
     for i in range(2):
-        if i == 1:
-            copy.wait()
-        for other, device in others:
-            send(6 + i, sums_s.at[i, other], sums_r.at[i, chip], device)
-        sums_r[i, chip] = sums_s[i, chip]
-
-    total = jnp.zeros((owned, width), F32)
-    for i in range(2):
-        arrived(6 + i, sums_r.at[i, pl.ds(0, chips - 1)])
         high, rest = halves(decode(sums_r[i].reshape(sources, width)))
         total = total + dot(deposits[i], high) + dot(deposits[i], rest)
-    part_s[...] = total.reshape(nrep, owned // nrep, width)
+    total = total.reshape(nrep, owned // nrep, width)
+    part_s[...] = encode(total, PART_CODES).astype(I32).astype(I16)
+    part_v[...] = total
     for other, device in reps:
         send(8, part_s.at[other], part_r.at[r], device)
-    part_r[r] = part_s[r]
+    part_r[r] = jnp.zeros(part_r.shape[1:], I16)
     arrived(8, part_r.at[pl.ds(0, nrep - 1)])
-    total = part_r[0]
-    for k in range(1, nrep):
-        total = total + part_r[k]
+    total = part_v[r]
+    for k in range(nrep):
+        total = total + decode(part_r[k], PART_CODES)
     source_ref[...] = total
     for copy in outputs:
         copy.wait()
@@ -427,7 +434,8 @@
             pltpu.VMEM((2, chips, 2, width), I16),
             pltpu.VMEM((2, chips, 2, width), I16),
             pltpu.VMEM((nrep, owned // nrep, width), F32),
-            pltpu.VMEM((nrep, owned // nrep, width), F32),
+            pltpu.VMEM((nrep, owned // nrep, width), I16),
+            pltpu.VMEM((nrep, owned // nrep, width), I16),
             pltpu.SemaphoreType.DMA((7,)),
             pltpu.SemaphoreType.DMA((2,)),
             pltpu.SemaphoreType.DMA((9,)),

time: 55.3 us -> 54.5 us (0.986)
  no operation moved by 1% of the time
where the time goes in v6:
time: 54.5 us; the launch traced here: 54.4 us
  Pallas kernels  53.1 us (97%)
  between operations  1.29 us (2%)
    pallas_call x1, Pallas kernels, per_device(): pl.pallas_call(functools.partial(step_kernel, ny, nz, nrep), out_shape=(j...  51.4 us
    pallas_call x1, Pallas kernels, per_device(): pl.pallas_call(functools.partial(hand_over, 3), out_shape=tuple((jax.Shap...  1.69 us

profile of v6, /device:TPU:1, one launch (start us, length us, event | category | flops | bytes accessed | tf_op | source)
XLA Modules:
  0.0 54.4 jit_solution(8282694459014734435)
XLA Ops:
  1.3 51.4 %parcel_step.1 = (f32[3,128,128]{2,1,0:T(8,128)}, f32[128,128]{1,0:T(8,128)}, f32[64,256]{1,0:T(8,128)}) custom-call(s32[1,128]{1,0:T(1,128)} %bitcast.5, s32[1,128]{1,0:T(1,128)} %bitcast.6, s32[1]{0:T(128)S(6)} %copy.11.busy_ref, bf16[256,256]{1,0:T(8,128)(2,1)} %field_hbm.1, bf16[128,64,128]{2,1,0:T(8,128)(2,1)} %tiles_hbm.1, f32[3,128,128]{2,1,0:T(8,128)} %bitcast.4, ...), custom_call_target="tpu_custom_call" | custom-call | tf_op jit(solution)/shard_map/parcel_step/pallas_call | solution.py:409
  52.7 1.7 %hand_over.1 = (f32[3,128,128]{2,1,0:T(8,128)}, f32[128,128]{1,0:T(8,128)}, f32[64,256]{1,0:T(8,128)}) custom-call(f32[3,128,128]{2,1,0:T(8,128)} %get-tuple-element.9.refs_0_, f32[128,128]{1,0:T(8,128)} %get-tuple-element.10.refs_1_, f32[64,256]{1,0:T(8,128)} %get-tuple-element.11.refs_2_), custom_call_target="tpu_custom_call" | custom-call | tf_op jit(solution)/shard_map/hand_over/pallas_call | solution.py:458

commit v7 on v6

--- a/solution.py
+++ b/solution.py
@@ -93,7 +93,7 @@
     sums_x,
     sums_s,
     sums_r,
-    part_v,
+    deposits,
     part_s,
     part_r,
     in_sem,
@@ -126,9 +126,9 @@
         others.append((other, {"cells": other * 2 + core, "rep": r}))
     sibling = {"cells": chip * 2 + (1 - core), "rep": r}
     reps = []
-    for step in range(1, nrep):
+    for step in sorted(range(nrep), key=lambda step: -min(step, nrep - step)):
         other = (r + step) & (nrep - 1)
-        reps.append((other, {"cells": me, "rep": other}))
+        reps.append((step, other, {"cells": me, "rep": other}))
 
     inputs = [
         pltpu.make_async_copy(src, dst, in_sem.at[i])
@@ -148,7 +148,8 @@
         copy.start()
 
     barrier = pltpu.get_barrier_semaphore()
-    for device in [device for _, device in others + reps] + [sibling]:
+    peers = [device for _, device in others] + [device for _, _, device in reps[:-1]]
+    for device in peers + [sibling]:
         pl.semaphore_signal(barrier, inc=1, device_id=device, device_id_type=MESH)
     for copy in inputs[3:]:
         copy.start()
@@ -230,23 +231,29 @@
     table = spread_out(lab_all)
     field_lane = iota((1, owned), 1).astype(F32)
 
+    def serve(i, wanted, field):
+        picks = jnp.where(field_lane == wanted, 1.0, 0.0).astype(BF16)
+        row_s[i] = dot(picks, field[...]).astype(BF16).reshape(chips, 2, width)
+
+    far, near = others[: len(others) // 4], others[len(others) // 4 :]
     here = find(table, me)
+    serve(0, here, field_v)
+    for other, device in far:
+        send(3, row_s.at[0, other], row_r.at[0, chip], device)
     place = find(table, chip * 2 + (1 - core))
     fields.wait()
-    for i, (wanted, field) in enumerate(((here, field_v), (place, field_x))):
-        picks = jnp.where(field_lane == wanted, 1.0, 0.0).astype(BF16)
-        row_s[i] = dot(picks, field[...]).astype(BF16).reshape(chips, 2, width)
-    for other, device in others:
+    serve(1, place, field_x)
+    for other, device in far:
+        send(3, row_s.at[1, other], row_r.at[1, chip], device)
+    for other, device in near:
         send(3, row_s.at[:, other], row_r.at[:, chip], device)
     row_r[:, chip] = row_s[:, chip]
 
     labels.wait()
-    deposits = []
-    for place in (here, find(spread_out(lab_x), me)):
-        deposits.append(
-            jnp.where(
-                iota((owned, 1), 0).astype(F32) == to_row(place), 1.0, 0.0
-            ).astype(BF16)
+    for i, place in enumerate((here, find(spread_out(lab_x), me))):
+        lines = jnp.where(iota((owned, 1), 0).astype(F32) == to_row(place), 1.0, 0.0)
+        deposits[:, :, i * sources : (i + 1) * sources] = lines.astype(BF16).reshape(
+            nrep, owned // nrep, sources
         )
     arrived(3, row_r.at[:, pl.ds(0, chips - 1)])
 
@@ -349,20 +356,16 @@
         send(6, sums_s.at[:, other], sums_r.at[:, chip], device)
     sums_r[:, chip] = sums_s[:, chip]
 
-    total = jnp.zeros((owned, width), F32)
     arrived(6, sums_r.at[:, pl.ds(0, chips - 1)])
-    for i in range(2):
-        high, rest = halves(decode(sums_r[i].reshape(sources, width)))
-        total = total + dot(deposits[i], high) + dot(deposits[i], rest)
-    total = total.reshape(nrep, owned // nrep, width)
-    part_s[...] = encode(total, PART_CODES).astype(I32).astype(I16)
-    part_v[...] = total
-    for other, device in reps:
-        send(8, part_s.at[other], part_r.at[r], device)
-    part_r[r] = jnp.zeros(part_r.shape[1:], I16)
-    arrived(8, part_r.at[pl.ds(0, nrep - 1)])
-    total = part_v[r]
-    for k in range(nrep):
+    high, rest = halves(decode(sums_r[...].reshape(slots, width)))
+    for step, other, device in reps:
+        lines = deposits[other]
+        total = dot(lines, high) + dot(lines, rest)
+        if step:
+            part_s[step - 1] = encode(total, PART_CODES).astype(I32).astype(I16)
+            send(8, part_s.at[step - 1], part_r.at[step - 1], device)
+    arrived(8, part_r)
+    for k in range(nrep - 1):
         total = total + decode(part_r[k], PART_CODES)
     source_ref[...] = total
     for copy in outputs:
@@ -433,9 +436,9 @@
             pltpu.VMEM((chips, 2, width), I16),
             pltpu.VMEM((2, chips, 2, width), I16),
             pltpu.VMEM((2, chips, 2, width), I16),
-            pltpu.VMEM((nrep, owned // nrep, width), F32),
-            pltpu.VMEM((nrep, owned // nrep, width), I16),
-            pltpu.VMEM((nrep, owned // nrep, width), I16),
+            pltpu.VMEM((nrep, owned // nrep, 4 * chips), BF16),
+            pltpu.VMEM((nrep - 1, owned // nrep, width), I16),
+            pltpu.VMEM((nrep - 1, owned // nrep, width), I16),
             pltpu.SemaphoreType.DMA((7,)),
             pltpu.SemaphoreType.DMA((2,)),
             pltpu.SemaphoreType.DMA((9,)),

time: 54.5 us -> 54.4 us (level)
  no operation moved by 1% of the time
where the time goes in v7:
time: 54.4 us; the launch traced here: 54.3 us
  Pallas kernels  53 us (97%)
  between operations  1.29 us (2%)
    pallas_call x1, Pallas kernels, per_device(): pl.pallas_call(functools.partial(step_kernel, ny, nz, nrep), out_shape=(j...  51.3 us
    pallas_call x1, Pallas kernels, per_device(): pl.pallas_call(functools.partial(hand_over, 3), out_shape=tuple((jax.Shap...  1.69 us

profile of v7, /device:TPU:1, one launch (start us, length us, event | category | flops | bytes accessed | tf_op | source)
XLA Modules:
  0.0 54.3 jit_solution(3975489336766629236)
XLA Ops:
  1.3 51.3 %parcel_step.1 = (f32[3,128,128]{2,1,0:T(8,128)}, f32[128,128]{1,0:T(8,128)}, f32[64,256]{1,0:T(8,128)}) custom-call(s32[1,128]{1,0:T(1,128)} %bitcast.5, s32[1,128]{1,0:T(1,128)} %bitcast.6, s32[1]{0:T(128)S(6)} %copy.11.busy_ref, bf16[256,256]{1,0:T(8,128)(2,1)} %field_hbm.1, bf16[128,64,128]{2,1,0:T(8,128)(2,1)} %tiles_hbm.1, f32[3,128,128]{2,1,0:T(8,128)} %bitcast.4, ...), custom_call_target="tpu_custom_call" | custom-call | tf_op jit(solution)/shard_map/parcel_step/pallas_call | solution.py:412
  52.6 1.7 %hand_over.1 = (f32[3,128,128]{2,1,0:T(8,128)}, f32[128,128]{1,0:T(8,128)}, f32[64,256]{1,0:T(8,128)}) custom-call(f32[3,128,128]{2,1,0:T(8,128)} %get-tuple-element.9.refs_0_, f32[128,128]{1,0:T(8,128)} %get-tuple-element.10.refs_1_, f32[64,256]{1,0:T(8,128)} %get-tuple-element.11.refs_2_), custom_call_target="tpu_custom_call" | custom-call | tf_op jit(solution)/shard_map/hand_over/pallas_call | solution.py:461
